TPU v7x, 1024 devices: a whole 8x8x8 slice. The times are simulated.
1024 devices in a mesh: oy: 16 (over y, core), ox: 64 (over x, z).
Axes of the slice: x: 8, y: 8, z: 8, core: 2. Of those that a mesh axis runs over, the one named last changes fastest.
Arguments:
- atm_flux: bfloat16 [4, 16, 49152], P(None, 'oy', 'ox'), may hold values from -6 to 6
- remap_weight: bfloat16 [16, 3584, 128, 128], P('oy', 'ox'), may hold values from -0.5 to 0.5
- source_block: int32 [16, 3584], P('oy', 'ox'), may hold values from 0 to 5
- send_counts: int32 [16, 448], P('oy', 'ox'), may hold values from 4 to 8, as said below
- recv_rows: int32 [16, 3584], P('oy', 'ox'), may hold values from 0 to 15, as said below
- land_mask: int32 [256, 8192], P('oy', 'ox'), may hold values 0 or 1
- tracers: float32 [3, 4, 256, 8192], P(None, None, 'oy', 'ox'), may hold values from -6 to 6
- east_velocity: float32 [4, 256, 8192], P(None, 'oy', 'ox'), may hold values from -0.2 to 0.2
- north_velocity: float32 [4, 256, 8192], P(None, 'oy', 'ox'), may hold values from -0.2 to 0.2
Outputs:
- ocean_flux: float32 [4, 256, 8192], P(None, 'oy', 'ox')
- new_tracers: float32 [3, 4, 256, 8192], P(None, None, 'oy', 'ox')
Inputs may be any that keep to these rules, and one draw needn't show every extreme that they name: send_counts[y, x * 7 + g] counts the first slots of group g that are live; every draw has a device that receives 8 live blocks from each of its 7 sources. `recv_rows`: for every receiving device, the slots with c < 4 name every row of its tile.
All inputs are finite; a program needn't handle non-finite values. No bound on the sum of `land_mask` on one device may be relied on, other than what follows from the above.
Results may differ from a plain program's by a relative error of at most 0.015.
Values sent between devices are 32-bit elements; how exact they have to be, the bound alone decides.
A program may use at most 32 MiB of HBM per device.

v0:
```python
import jax
import jax.numpy as jnp
from jax import lax
from jax.sharding import PartitionSpec as P

STEPS = 2
REACH = 3
CAP = 8


lateral_mixing = 0.08
vertical_mixing = 0.1
surface_gain = 0.5


def from_behind(x, axis, by):
    devices = lax.axis_size(axis)
    return lax.ppermute(x, axis, [(i, (i + by) % devices) for i in range(devices)])


def padded_2(cells, sides, width):
    for axis, dim in sides:
        count = lax.axis_size(axis)
        head = lax.slice_in_dim(cells, 0, width, axis=dim)
        tail = lax.slice_in_dim(cells, cells.shape[dim] - width, cells.shape[dim], axis=dim)
        cells = jnp.concatenate(
            [
                lax.ppermute(tail, axis, [(i, (i + 1) % count) for i in range(count)]),
                cells,
                lax.ppermute(head, axis, [((i + 1) % count, i) for i in range(count)]),
            ],
            axis=dim,
        )
    return cells


def tendency_step(padded, wet_padded, eastward, northward, kv_top, source):
    center = padded[..., 1:-1, 1:-1]
    east_side = padded[..., 1:-1, 2:]
    west_side = padded[..., 1:-1, :-2]
    north_side = padded[..., 2:, 1:-1]
    south_side = padded[..., :-2, 1:-1]
    wet = wet_padded[1:-1, 1:-1]
    advect = jnp.maximum(eastward, 0.0) * (center - west_side) + jnp.minimum(eastward, 0.0) * (
        east_side - center
    )
    advect = (
        advect
        + jnp.maximum(northward, 0.0) * (center - south_side)
        + jnp.minimum(northward, 0.0) * (north_side - center)
    )
    spread = lateral_mixing * (
        wet_padded[1:-1, 2:] * (east_side - center)
        + wet_padded[1:-1, :-2] * (west_side - center)
        + wet_padded[2:, 1:-1] * (north_side - center)
        + wet_padded[:-2, 1:-1] * (south_side - center)
    )
    faces = jnp.concatenate(
        [
            kv_top[None, None] * (center[:, 1:2] - center[:, 0:1]),
            vertical_mixing * (center[:, 2:] - center[:, 1:-1]),
        ],
        axis=1,
    )
    zeros = jnp.zeros_like(center[:, :1])
    vdiff = jnp.concatenate([faces, zeros], axis=1) - jnp.concatenate([zeros, faces], axis=1)
    surface = jnp.concatenate([source[:, None], jnp.zeros_like(center[:, 1:])], axis=1)
    return center + wet * (-advect + spread + vdiff + surface)


def forcing(flux_fields, tracer_count):
    mixing = flux_fields[flux_fields.shape[0] - 1]
    kv_top = 0.05 + 0.15 * mixing * mixing / (1.0 + mixing * mixing)
    return (kv_top, surface_gain * flux_fields[:tracer_count])


def clear_rim(padded, width):
    row_index = lax.axis_index("oy")
    row_count = lax.axis_size("oy")
    rows = jnp.arange(padded.shape[1])
    drop = (rows < width) & (row_index == 0) | (rows >= padded.shape[1] - width) & (
        row_index == row_count - 1
    )
    return padded * jnp.where(drop, 0.0, 1.0).astype(jnp.float32)[:, None]


def body(
    atm_flux,
    remap_weight,
    source_block,
    send_counts,
    recv_rows,
    land_mask,
    tracers,
    east_velocity,
    north_velocity,
):
    flux_count = atm_flux.shape[0]
    block_cols = remap_weight.shape[2]
    tile_cols = remap_weight.shape[3]
    slot_count = remap_weight.shape[1]
    group_count = send_counts.shape[1]
    block_count = atm_flux.shape[2] // block_cols
    tracer_count, level_count, tile_rows = (tracers.shape[0], tracers.shape[1], tracers.shape[2])
    flux_blocks = atm_flux[:, 0].reshape(flux_count, block_count, block_cols)
    picker = (source_block[0][:, None] == jnp.arange(block_count)[None, :]).astype(jnp.bfloat16)
    chosen = jnp.einsum(
        "sn,fnb->sfb", picker, flux_blocks, preferred_element_type=jnp.float32
    ).astype(jnp.bfloat16)
    partial_value = jnp.einsum(
        "sfb,sbc->sfc", chosen, remap_weight[0], preferred_element_type=jnp.float32
    )
    slot = jnp.arange(slot_count)
    live = slot % CAP < send_counts[0][slot // CAP]
    groups = (partial_value * live.astype(jnp.float32)[:, None, None]).reshape(
        group_count, CAP * flux_count * tile_cols
    )
    pieces = []
    for group in range(group_count):
        offset = group - REACH
        if offset == 0:
            pieces.append(groups[group])
        else:
            pieces.append(from_behind(groups[group], "ox", offset))
    gathered = jnp.stack(pieces, axis=0)
    gathered = gathered.reshape(slot_count, flux_count, tile_cols)
    placer = (recv_rows[0][:, None] == jnp.arange(tile_rows)[None, :]).astype(jnp.float32)
    ocean_flux = jnp.einsum("st,sfc->ftc", placer, gathered, precision=lax.Precision.HIGHEST)
    wet = land_mask.astype(jnp.float32)
    kv_top, source = forcing(ocean_flux, tracer_count)
    fields = tracer_count * level_count
    state = tracers
    for step in range(STEPS):
        stacked = jnp.concatenate([state.reshape(fields, tile_rows, tile_cols), wet[None]], axis=0)
        padded = padded_2(stacked, (("oy", 1), ("ox", 2)), 1)
        padded = clear_rim(padded, 1)
        state_padded = padded[:fields].reshape(
            tracer_count, level_count, tile_rows + 2, tile_cols + 2
        )
        state = tendency_step(
            state_padded, padded[fields], east_velocity[None], north_velocity[None], kv_top, source
        )
    return (ocean_flux, state)


def solution(mesh):
    in_specs = (
        P(None, "oy", "ox"),
        P("oy", "ox", None, None),
        P("oy", "ox"),
        P("oy", "ox"),
        P("oy", "ox"),
        P("oy", "ox"),
        P(None, None, "oy", "ox"),
        P(None, "oy", "ox"),
        P(None, "oy", "ox"),
    )
    out_specs = (P(None, "oy", "ox"), P(None, None, "oy", "ox"))
    return jax.shard_map(body, mesh=mesh, in_specs=in_specs, out_specs=out_specs, check_vma=False)
```

profile of v0, /device:TPU:57, one launch (start us, length us, event | category | flops | bytes accessed | tf_op | source)
XLA Modules:
  0.0 84.7 jit_solution(17156731598730496613)
XLA Ops:
  0.6 0.0 copy-start
  0.6 0.0 copy-start.1
  0.7 0.0 copy-start.3
  0.7 0.0 copy-start.4
  0.7 0.8 convert_bitcast_fusion
  1.5 0.8 fusion.46
  2.3 3.2 %collective-permute-start.6 = (f32[13,1,128]{2,1,0:T(1,128)S(1)}, f32[13,1,128]{2,1,0:T(1,128)S(1)}, u32[]{:S(2)}, u32[]{:S(2)}) collective-permute-start(f32[13,1,128]{2,1,0:T(1,128)S(1)} %get-tuple-element.33), channel_id=1, source_target_pairs={{0,64},{64,128},{128,192},{192,256},{256,320},{320,384},{384,448},... | collective-permute-start | bytes 19976 | tf_op jit(solution)/shard_map/ppermute | solution.py:28
  5.5 0.0 collective-permute-start.7
  5.5 1.6 %fusion.58 = (s32[1,1]{1,0:T(1,128)}, s32[1,1]{1,0:T(1,128)}, s32[1,1]{1,0:T(1,128)}, s32[1,1]{1,0:T(1,128)}, s32[1,1]{1,0:T(1,128)}, /*index=5*/s32[1,1]{1,0:T(1,128)}, s32[1,1]{1,0:T(1,128)}) fusion(s32[1,7]{1,0:T(1,128)} %param.12), kind=kLoop, calls=%fused_computation.107 | loop fusion | bytes 56 | tf_op jit(solution)/shard_map/gather | solution.py:114
  7.1 0.7 reshape_squeeze.3
  7.8 0.8 %fusion.33 = bf16[56,4,128]{2,0,1:T(8,128)(2,1)S(1)} fusion(bf16[4,6,128]{2,1,0:T(8,128)(2,1)S(1)} %reshape_squeeze.3, s32[56]{0:T(128)} %bitcast.103), kind=kOutput, calls=%fused_computation.53 | convolution fusion | flops 344400 | bytes 63712 | tf_op jit(solution)/shard_map/sn,fnb->sfb/dot_general | solution.py:107
  8.7 4.3 %compare_convert_fusion = f32[56]{0:T(128)S(1)} fusion(s32[]{:T(128)} %bitcast.3, s32[]{:T(128)} %bitcast.4, s32[]{:T(128)} %bitcast.5, s32[]{:T(128)} %bitcast.6, s32[]{:T(128)} %bitcast.7, s32[]{:T(128)} %bitcast.9, s32[]{:T(128)} %bitcast.8), kind=kLoop, calls=%fused_computation.91 | loop fusion | flops 1736 | bytes 252 | tf_op jit(solution)/shard_map/convert_element_type | solution.py:115
  13.0 0.0 copy-done
  13.0 0.6 fusion.2
  13.6 7.6 %collective-permute-start.4 = (f32[4096]{0:T(1024)S(1)}, f32[4096]{0:T(1024)S(1)}, u32[]{:S(2)}, u32[]{:S(2)}) collective-permute-start(f32[4096]{0:T(1024)S(1)} %bitcast.96), channel_id=1, source_target_pairs={{0,2},{1,3},{2,4},{3,5},{4,6},{5,7},{6,8},{7,9},{8,10},{9,11},{10,... | collective-permute-start | bytes 49160 | tf_op jit(solution)/shard_map/ppermute | solution.py:18
  21.3 10.7 %collective-permute-start.5 = (f32[4096]{0:T(1024)S(1)}, f32[4096]{0:T(1024)S(1)}, u32[]{:S(2)}, u32[]{:S(2)}) collective-permute-start(f32[4096]{0:T(1024)S(1)} %bitcast.95), channel_id=1, source_target_pairs={{0,3},{1,4},{2,5},{3,6},{4,7},{5,8},{6,9},{7,10},{8,11},{9,12},{10... | collective-permute-start | bytes 49160 | tf_op jit(solution)/shard_map/ppermute | solution.py:18
  31.9 4.0 %collective-permute-start.3 = (f32[4096]{0:T(1024)S(1)}, f32[4096]{0:T(1024)S(1)}, u32[]{:S(2)}, u32[]{:S(2)}) collective-permute-start(f32[4096]{0:T(1024)S(1)} %bitcast.94), channel_id=1, source_target_pairs={{0,1},{1,2},{2,3},{3,4},{4,5},{5,6},{6,7},{7,8},{8,9},{9,10},{10,1... | collective-permute-start | bytes 49160 | tf_op jit(solution)/shard_map/ppermute | solution.py:18
  36.0 0.0 copy-done.3
  36.0 0.0 copy-done.4
  36.0 0.0 collective-permute-done.6
  36.0 0.0 collective-permute-done.7
  36.0 0.0 copy-done.1
  36.1 0.0 copy-start.5
  36.1 0.1 fusion.54
  36.2 4.0 %collective-permute-start.8 = (f32[13,18,1]{2,1,0:T(8,128)S(1)}, f32[13,18,1]{2,1,0:T(8,128)S(1)}, u32[]{:S(2)}, u32[]{:S(2)}) collective-permute-start(f32[13,18,1]{2,1,0:T(8,128)S(1)} %get-tuple-element.22), channel_id=1, source_target_pairs={{0,1},{1,2},{2,3},{3,4},{4,5},{5,6},{6,7},{7,8},{8,9},{9,10},{10,1... | collective-permute-start | bytes 2816 | tf_op jit(solution)/shard_map/ppermute | solution.py:28
  40.2 4.6 %collective-permute-start.9 = (f32[13,18,1]{2,1,0:T(8,128)S(1)}, f32[13,18,1]{2,1,0:T(8,128)S(1)}, u32[]{:S(2)}, u32[]{:S(2)}) collective-permute-start(f32[13,18,1]{2,1,0:T(8,128)S(1)} %get-tuple-element.23), channel_id=1, source_target_pairs={{1,0},{2,1},{3,2},{4,3},{5,4},{6,5},{7,6},{8,7},{9,8},{10,9},{11,1... | collective-permute-start | bytes 2816 | tf_op jit(solution)/shard_map/ppermute | solution.py:30
  44.8 2.3 %collective-permute-done.8 = f32[13,18,1]{2,1,0:T(8,128)S(1)} collective-permute-done((f32[13,18,1]{2,1,0:T(8,128)S(1)}, f32[13,18,1]{2,1,0:T(8,128)S(1)}, u32[]{:S(2)}, u32[]{:S(2)}) %collective-permute-start.8) | collective-permute-done | bytes 968 | tf_op jit(solution)/shard_map/ppermute | solution.py:28
  47.1 1.9 %collective-permute-start.2 = (f32[4096]{0:T(1024)S(1)}, f32[4096]{0:T(1024)S(1)}, u32[]{:S(2)}, u32[]{:S(2)}) collective-permute-start(f32[4096]{0:T(1024)S(1)} %bitcast.93), channel_id=1, source_target_pairs={{0,63},{1,0},{2,1},{3,2},{4,3},{5,4},{6,5},{7,6},{8,7},{9,8},{10,9... | collective-permute-start | bytes 49160 | tf_op jit(solution)/shard_map/ppermute | solution.py:18
  49.0 0.0 collective-permute-done.9
  49.0 3.1 %collective-permute-start.1 = (f32[4096]{0:T(1024)S(1)}, f32[4096]{0:T(1024)S(1)}, u32[]{:S(2)}, u32[]{:S(2)}) collective-permute-start(f32[4096]{0:T(1024)S(1)} %bitcast.92), channel_id=1, source_target_pairs={{0,62},{1,63},{2,0},{3,1},{4,2},{5,3},{6,4},{7,5},{8,6},{9,7},{10,... | collective-permute-start | bytes 49160 | tf_op jit(solution)/shard_map/ppermute | solution.py:18
  52.1 0.3 fusion.9
  52.4 0.1 fusion.52
  52.5 0.2 fusion.51
  52.7 0.0 collective-permute-done.4
  52.7 3.1 %collective-permute-start = (f32[4096]{0:T(1024)S(1)}, f32[4096]{0:T(1024)S(1)}, u32[]{:S(2)}, u32[]{:S(2)}) collective-permute-start(f32[4096]{0:T(1024)S(1)} %bitcast.91), channel_id=1, source_target_pairs={{0,61},{1,62},{2,63},{3,0},{4,1},{5,2},{6,3},{7,4},{8,5},{9,6},{10... | collective-permute-start | bytes 49160 | tf_op jit(solution)/shard_map/ppermute | solution.py:18
  55.8 0.1 fusion.57
  55.9 0.0 collective-permute-done.5
  55.9 0.0 collective-permute-done.3
  55.9 0.0 collective-permute-done.2
  55.9 0.0 collective-permute-done.1
  55.9 3.1 %collective-permute-done = f32[4096]{0:T(1024)S(1)} collective-permute-done((f32[4096]{0:T(1024)S(1)}, f32[4096]{0:T(1024)S(1)}, u32[]{:S(2)}, u32[]{:S(2)}) %collective-permute-start) | collective-permute-done | bytes 16416 | tf_op jit(solution)/shard_map/ppermute | solution.py:18
  59.0 0.2 stack.27
  59.2 0.1 reshape.137
  59.3 0.0 copy-done.5
  59.3 0.2 convolution_bitcast_fusion
  59.5 0.1 fusion.39
  59.6 0.1 fusion.21
  59.7 4.9 %collective-permute-start.10 = (f32[13,1,128]{2,1,0:T(1,128)S(1)}, f32[13,1,128]{2,1,0:T(1,128)S(1)}, u32[]{:S(2)}, u32[]{:S(2)}) collective-permute-start(f32[13,1,128]{2,1,0:T(1,128)S(1)} %get-tuple-element.31), channel_id=1, source_target_pairs={{0,64},{64,128},{128,192},{192,256},{256,320},{320,384},{384,448},... | collective-permute-start | bytes 19976 | tf_op jit(solution)/shard_map/ppermute | solution.py:28
  64.6 0.0 collective-permute-start.11
  64.6 0.8 collective-permute-done.10
  65.4 3.5 %collective-permute-done.11 = f32[13,1,128]{2,1,0:T(1,128)S(1)} collective-permute-done((f32[13,1,128]{2,1,0:T(1,128)S(1)}, f32[13,1,128]{2,1,0:T(1,128)S(1)}, u32[]{:S(2)}, u32[]{:S(2)}) %collective-permute-start.11) | collective-permute-done | bytes 6688 | tf_op jit(solution)/shard_map/ppermute | solution.py:30
  68.9 0.1 fusion.53
  69.0 8.1 %collective-permute-start.12 = (f32[13,18,1]{2,1,0:T(8,128)S(1)}, f32[13,18,1]{2,1,0:T(8,128)S(1)}, u32[]{:S(2)}, u32[]{:S(2)}) collective-permute-start(f32[13,18,1]{2,1,0:T(8,128)S(1)} %get-tuple-element.20), channel_id=1, source_target_pairs={{0,1},{1,2},{2,3},{3,4},{4,5},{5,6},{6,7},{7,8},{8,9},{9,10},{10,1... | collective-permute-start | bytes 2816 | tf_op jit(solution)/shard_map/ppermute | solution.py:28
  77.2 2.6 %collective-permute-start.13 = (f32[13,18,1]{2,1,0:T(8,128)S(1)}, f32[13,18,1]{2,1,0:T(8,128)S(1)}, u32[]{:S(2)}, u32[]{:S(2)}) collective-permute-start(f32[13,18,1]{2,1,0:T(8,128)S(1)} %get-tuple-element.21), channel_id=1, source_target_pairs={{1,0},{2,1},{3,2},{4,3},{5,4},{6,5},{7,6},{8,7},{9,8},{10,9},{11,1... | collective-permute-start | bytes 2816 | tf_op jit(solution)/shard_map/ppermute | solution.py:30
  79.8 0.7 collective-permute-done.12
  80.5 2.7 %collective-permute-done.13 = f32[13,18,1]{2,1,0:T(8,128)S(1)} collective-permute-done((f32[13,18,1]{2,1,0:T(8,128)S(1)}, f32[13,18,1]{2,1,0:T(8,128)S(1)}, u32[]{:S(2)}, u32[]{:S(2)}) %collective-permute-start.13) | collective-permute-done | bytes 968 | tf_op jit(solution)/shard_map/ppermute | solution.py:30
  83.2 0.2 fusion.14
  83.5 0.0 copy-done.2
  83.5 0.1 fusion.36
  83.6 0.1 fusion.50
  83.7 0.2 fusion.49
  83.9 0.1 fusion.56
  83.9 0.1 fusion.23
  84.1 0.6 copy.34
  (17 shorter events, 0.2 us)
Async XLA Ops:
  0.6 12.4 %copy-start = (bf16[1,56,128,128]{3,2,1,0:T(8,128)(2,1)S(1)}, bf16[1,56,128,128]{3,2,1,0:T(8,128)(2,1)}, u32[]{:S(2)}) copy-start(bf16[1,56,128,128]{3,2,1,0:T(8,128)(2,1)} %param.10) | copy-start | bytes 5505028
  0.6 35.4 %copy-start.1 = (f32[3,4,16,128]{3,2,1,0:T(8,128)S(1)}, f32[3,4,16,128]{3,2,1,0:T(8,128)}, u32[]{:S(2)}) copy-start(f32[3,4,16,128]{3,2,1,0:T(8,128)} %param.15) | copy-start | bytes 294916
  0.7 35.3 %copy-start.3 = (f32[4,16,128]{2,1,0:T(8,128)S(1)}, f32[4,16,128]{2,1,0:T(8,128)}, u32[]{:S(2)}) copy-start(f32[4,16,128]{2,1,0:T(8,128)} %param.17) | copy-start | bytes 98308
  0.7 35.3 %copy-start.4 = (f32[4,16,128]{2,1,0:T(8,128)S(1)}, f32[4,16,128]{2,1,0:T(8,128)}, u32[]{:S(2)}) copy-start(f32[4,16,128]{2,1,0:T(8,128)} %param.16) | copy-start | bytes 98308
  2.3 33.7 %collective-permute-start.6 = (f32[13,1,128]{2,1,0:T(1,128)S(1)}, f32[13,1,128]{2,1,0:T(1,128)S(1)}, u32[]{:S(2)}, u32[]{:S(2)}) collective-permute-start(f32[13,1,128]{2,1,0:T(1,128)S(1)} %get-tuple-element.33), channel_id=1, source_target_pairs={{0,64},{64,128},{128,192},{192,256},{256,320},{320,384},{384,448},... | collective-permute-start | bytes 19976 | tf_op jit(solution)/shard_map/ppermute | solution.py:28
  5.5 30.5 %collective-permute-start.7 = (f32[13,1,128]{2,1,0:T(1,128)S(1)}, f32[13,1,128]{2,1,0:T(1,128)S(1)}, u32[]{:S(2)}, u32[]{:S(2)}) collective-permute-start(f32[13,1,128]{2,1,0:T(1,128)S(1)} %get-tuple-element.34), channel_id=1, source_target_pairs={{64,0},{128,64},{192,128},{256,192},{320,256},{384,320},{448,384},... | collective-permute-start | bytes 19976 | tf_op jit(solution)/shard_map/ppermute | solution.py:30
  13.6 39.1 %collective-permute-start.4 = (f32[4096]{0:T(1024)S(1)}, f32[4096]{0:T(1024)S(1)}, u32[]{:S(2)}, u32[]{:S(2)}) collective-permute-start(f32[4096]{0:T(1024)S(1)} %bitcast.96), channel_id=1, source_target_pairs={{0,2},{1,3},{2,4},{3,5},{4,6},{5,7},{6,8},{7,9},{8,10},{9,11},{10,... | collective-permute-start | bytes 49160 | tf_op jit(solution)/shard_map/ppermute | solution.py:18
  21.3 34.6 %collective-permute-start.5 = (f32[4096]{0:T(1024)S(1)}, f32[4096]{0:T(1024)S(1)}, u32[]{:S(2)}, u32[]{:S(2)}) collective-permute-start(f32[4096]{0:T(1024)S(1)} %bitcast.95), channel_id=1, source_target_pairs={{0,3},{1,4},{2,5},{3,6},{4,7},{5,8},{6,9},{7,10},{8,11},{9,12},{10... | collective-permute-start | bytes 49160 | tf_op jit(solution)/shard_map/ppermute | solution.py:18
  31.9 23.9 %collective-permute-start.3 = (f32[4096]{0:T(1024)S(1)}, f32[4096]{0:T(1024)S(1)}, u32[]{:S(2)}, u32[]{:S(2)}) collective-permute-start(f32[4096]{0:T(1024)S(1)} %bitcast.94), channel_id=1, source_target_pairs={{0,1},{1,2},{2,3},{3,4},{4,5},{5,6},{6,7},{7,8},{8,9},{9,10},{10,1... | collective-permute-start | bytes 49160 | tf_op jit(solution)/shard_map/ppermute | solution.py:18
  36.1 23.2 %copy-start.5 = (s32[1,56]{1,0:T(1,128)S(1)}, s32[1,56]{1,0:T(1,128)}, u32[]{:S(2)}) copy-start(s32[1,56]{1,0:T(1,128)} %param.13) | copy-start | bytes 676
  36.2 10.9 %collective-permute-start.8 = (f32[13,18,1]{2,1,0:T(8,128)S(1)}, f32[13,18,1]{2,1,0:T(8,128)S(1)}, u32[]{:S(2)}, u32[]{:S(2)}) collective-permute-start(f32[13,18,1]{2,1,0:T(8,128)S(1)} %get-tuple-element.22), channel_id=1, source_target_pairs={{0,1},{1,2},{2,3},{3,4},{4,5},{5,6},{6,7},{7,8},{8,9},{9,10},{10,1... | collective-permute-start | bytes 2816 | tf_op jit(solution)/shard_map/ppermute | solution.py:28
  40.2 8.8 %collective-permute-start.9 = (f32[13,18,1]{2,1,0:T(8,128)S(1)}, f32[13,18,1]{2,1,0:T(8,128)S(1)}, u32[]{:S(2)}, u32[]{:S(2)}) collective-permute-start(f32[13,18,1]{2,1,0:T(8,128)S(1)} %get-tuple-element.23), channel_id=1, source_target_pairs={{1,0},{2,1},{3,2},{4,3},{5,4},{6,5},{7,6},{8,7},{9,8},{10,9},{11,1... | collective-permute-start | bytes 2816 | tf_op jit(solution)/shard_map/ppermute | solution.py:30
  47.1 8.8 %collective-permute-start.2 = (f32[4096]{0:T(1024)S(1)}, f32[4096]{0:T(1024)S(1)}, u32[]{:S(2)}, u32[]{:S(2)}) collective-permute-start(f32[4096]{0:T(1024)S(1)} %bitcast.93), channel_id=1, source_target_pairs={{0,63},{1,0},{2,1},{3,2},{4,3},{5,4},{6,5},{7,6},{8,7},{9,8},{10,9... | collective-permute-start | bytes 49160 | tf_op jit(solution)/shard_map/ppermute | solution.py:18
  49.0 6.9 %collective-permute-start.1 = (f32[4096]{0:T(1024)S(1)}, f32[4096]{0:T(1024)S(1)}, u32[]{:S(2)}, u32[]{:S(2)}) collective-permute-start(f32[4096]{0:T(1024)S(1)} %bitcast.92), channel_id=1, source_target_pairs={{0,62},{1,63},{2,0},{3,1},{4,2},{5,3},{6,4},{7,5},{8,6},{9,7},{10,... | collective-permute-start | bytes 49160 | tf_op jit(solution)/shard_map/ppermute | solution.py:18
  52.7 6.3 %collective-permute-start = (f32[4096]{0:T(1024)S(1)}, f32[4096]{0:T(1024)S(1)}, u32[]{:S(2)}, u32[]{:S(2)}) collective-permute-start(f32[4096]{0:T(1024)S(1)} %bitcast.91), channel_id=1, source_target_pairs={{0,61},{1,62},{2,63},{3,0},{4,1},{5,2},{6,3},{7,4},{8,5},{9,6},{10... | collective-permute-start | bytes 49160 | tf_op jit(solution)/shard_map/ppermute | solution.py:18
  59.4 24.0 %copy-start.2 = (f32[4,16,128]{2,1,0:T(8,128)}, f32[4,16,128]{2,1,0:T(8,128)S(1)}, u32[]{:S(2)}) copy-start(f32[4,16,128]{2,1,0:T(8,128)S(1)} %convolution_bitcast_fusion) | copy-start | bytes 98308
  59.7 5.7 %collective-permute-start.10 = (f32[13,1,128]{2,1,0:T(1,128)S(1)}, f32[13,1,128]{2,1,0:T(1,128)S(1)}, u32[]{:S(2)}, u32[]{:S(2)}) collective-permute-start(f32[13,1,128]{2,1,0:T(1,128)S(1)} %get-tuple-element.31), channel_id=1, source_target_pairs={{0,64},{64,128},{128,192},{192,256},{256,320},{320,384},{384,448},... | collective-permute-start | bytes 19976 | tf_op jit(solution)/shard_map/ppermute | solution.py:28
  64.6 4.3 %collective-permute-start.11 = (f32[13,1,128]{2,1,0:T(1,128)S(1)}, f32[13,1,128]{2,1,0:T(1,128)S(1)}, u32[]{:S(2)}, u32[]{:S(2)}) collective-permute-start(f32[13,1,128]{2,1,0:T(1,128)S(1)} %get-tuple-element.32), channel_id=1, source_target_pairs={{64,0},{128,64},{192,128},{256,192},{320,256},{384,320},{448,384},... | collective-permute-start | bytes 19976 | tf_op jit(solution)/shard_map/ppermute | solution.py:30
  69.0 11.4 %collective-permute-start.12 = (f32[13,18,1]{2,1,0:T(8,128)S(1)}, f32[13,18,1]{2,1,0:T(8,128)S(1)}, u32[]{:S(2)}, u32[]{:S(2)}) collective-permute-start(f32[13,18,1]{2,1,0:T(8,128)S(1)} %get-tuple-element.20), channel_id=1, source_target_pairs={{0,1},{1,2},{2,3},{3,4},{4,5},{5,6},{6,7},{7,8},{8,9},{9,10},{10,1... | collective-permute-start | bytes 2816 | tf_op jit(solution)/shard_map/ppermute | solution.py:28
  77.2 6.0 %collective-permute-start.13 = (f32[13,18,1]{2,1,0:T(8,128)S(1)}, f32[13,18,1]{2,1,0:T(8,128)S(1)}, u32[]{:S(2)}, u32[]{:S(2)}) collective-permute-start(f32[13,18,1]{2,1,0:T(8,128)S(1)} %get-tuple-element.21), channel_id=1, source_target_pairs={{1,0},{2,1},{3,2},{4,3},{5,4},{6,5},{7,6},{8,7},{9,8},{10,9},{11,1... | collective-permute-start | bytes 2816 | tf_op jit(solution)/shard_map/ppermute | solution.py:30
where the time goes:
time: 85.3 us; the launch traced here: 84.7 us
  starting transfers between devices  57.8 us (68%)
  waiting for transfers between devices  13.1 us (15%)
  other arithmetic  7.02 us (8%)
  local copies, waits for them, and re-layouts  4.17 us (5%)
  matrix products  1.58 us (2%)
  between operations  1.08 us (1%)
    ppermute x6, starting transfers between devices, from_behind(): lax.ppermute(x, axis, [(i, (i + by) % devices) for i in range(devices)])  30.4 us
    ppermute x4, starting transfers between devices, padded_2(): lax.ppermute(tail, axis, [(i, (i + 1) % count) for i in range(count)])  20.3 us
    ppermute x4, starting transfers between devices, padded_2(): lax.ppermute(head, axis, [((i + 1) % count, i) for i in range(count)])  7.18 us
    ppermute x4, waiting for transfers between devices, padded_2(): lax.ppermute(head, axis, [((i + 1) % count, i) for i in range(count)])  6.21 us
    convert_element_type x1, other arithmetic, body(): live.astype(jnp.float32)[:, None, None]  4.34 us
    ppermute x4, waiting for transfers between devices, padded_2(): lax.ppermute(tail, axis, [(i, (i + 1) % count) for i in range(count)])  3.75 us
    ppermute x6, waiting for transfers between devices, from_behind(): lax.ppermute(x, axis, [(i, (i + by) % devices) for i in range(devices)])  3.1 us
  transfers between devices with their start and end apart: 14, of which 6 were waited for; matrix products, arithmetic and copies ran while one was open for 10% of the time, Pallas kernels for 0%

commit v1 on v0

v1 whole, which is shorter than its diff:
```python
import jax
import jax.numpy as jnp
from jax import lax
from jax.experimental import pallas as pl
from jax.experimental.pallas import tpu as pltpu
from jax.sharding import PartitionSpec as P

MESH = pl.DeviceIdType.MESH
FLUX = 4
TRACERS = 3
LEVELS = 4
FIELDS = TRACERS * LEVELS
ROWS = 16
COLS = 128
BLOCKS = 6
REACH = 3
CAP = 8
GROUPS = 7
SLOTS = GROUPS * CAP
ORDER = (0, 6, 1, 5, 2, 4, 3)
NEAR = (1, 2, 3, 4, 5)
FAR = (0, 6)
LATERAL = 0.08
VERTICAL = 0.1
GAIN = 0.5
F32 = jnp.float32
BF16 = jnp.bfloat16


def lanes(shape):
    return lax.broadcasted_iota(jnp.int32, shape, len(shape) - 1)


def rows(shape):
    return lax.broadcasted_iota(jnp.int32, shape, len(shape) - 2)


def kernel(
    flux_h, weight_h, source_h, count_h, recv_h, land_h, tracer_h, east_h, north_h,
    ocean_o, new_o,
    flux_v, weight_v, source_v, count_v, place_v, land_v, tracer_v, east_v, north_v,
    lhs_v, send_v, recv_v, state_v, col_out, col_in, row_out, row_in,
    load_sem, weight_sem, part_send, part_recv, halo_send, halo_recv,
):
    oy, ox = lax.axis_index("oy"), lax.axis_index("ox")
    n_oy, n_ox = lax.axis_size("oy"), lax.axis_size("ox")

    def along(offset):
        return (oy, lax.rem(ox + (n_ox + offset), n_ox))

    up = (lax.rem(oy + 1, n_oy), ox)
    down = (lax.rem(oy + (n_oy - 1), n_oy), ox)

    loads = {}
    for i, (name, src, dst) in enumerate((
        ("tracer", tracer_h, tracer_v), ("land", land_h, land_v), ("flux", flux_h, flux_v),
        ("source", source_h, source_v), ("count", count_h, count_v), ("place", recv_h, place_v),
        ("east", east_h, east_v), ("north", north_h, north_v),
    )):
        loads[name] = pltpu.make_async_copy(src, dst, load_sem.at[i])
    weights = {
        g: pltpu.make_async_copy(
            weight_h.at[pl.ds(g * CAP, CAP)], weight_v.at[pl.ds(g * CAP, CAP)], weight_sem.at[g]
        )
        for g in range(GROUPS)
    }
    for name in ("tracer", "land", "flux", "source", "count"):
        loads[name].start()
    for g in ORDER:
        weights[g].start()
    for name in ("place", "east", "north"):
        loads[name].start()

    barrier = pltpu.get_barrier_semaphore()
    partners = [along(d) for d in (-3, 3, -2, 2, -1, 1)] + [up, down]
    for device in partners:
        pl.semaphore_signal(barrier, inc=1, device_id=device, device_id_type=MESH)

    def halo_copies(e):
        out = []
        for side, (src, dst, device) in enumerate((
            (row_out.at[e, 0], row_in.at[e, 0], down), (row_out.at[e, 1], row_in.at[e, 1], up),
            (col_out.at[e], col_in.at[e, 0], along(1)), (col_out.at[e], col_in.at[e, 1], along(-1)),
        )):
            out.append(pltpu.make_async_remote_copy(
                src_ref=src, dst_ref=dst, send_sem=halo_send.at[e, side], recv_sem=halo_recv.at[e, side],
                device_id=device, device_id_type=MESH,
            ))
        return out

    lane = lanes((ROWS, COLS))
    row = rows((ROWS, COLS))

    def pack(fields):
        packed = jnp.zeros((ROWS, COLS), F32)
        for k, field in enumerate(fields):
            packed = jnp.where((lane == 2 * k) | (lane == 2 * k + 1), pltpu.roll(field, 2 * k + 1, 1), packed)
        return packed

    def shift(x, by, axis):
        return pltpu.roll(x, by % x.shape[axis], axis)

    loads["tracer"].wait()
    loads["land"].wait()
    wet = land_v[...].astype(F32)
    first = [tracer_v[pl.ds(k * ROWS, ROWS), :] for k in range(FIELDS)]
    row_out[0, 0, 0:FIELDS, :] = tracer_v[pl.ds(0, FIELDS, stride=ROWS), :]
    row_out[0, 1, 0:FIELDS, :] = tracer_v[pl.ds(ROWS - 1, FIELDS, stride=ROWS), :]
    row_out[0, 0, FIELDS:ROWS, :] = jnp.broadcast_to(wet[0:1], (ROWS - FIELDS, COLS))
    row_out[0, 1, FIELDS:ROWS, :] = jnp.broadcast_to(wet[ROWS - 1 : ROWS], (ROWS - FIELDS, COLS))
    col_out[0] = pack(first + [wet])

    loads["flux"].wait()
    loads["source"].wait()
    loads["count"].wait()
    flux = flux_v[...].astype(F32)
    blocks = jnp.concatenate([flux[:, n * COLS : (n + 1) * COLS] for n in range(BLOCKS)], axis=0)
    blocks = jnp.concatenate([blocks, jnp.zeros((COLS - FLUX * BLOCKS, COLS), F32)], axis=0).astype(BF16)
    wide = FLUX * SLOTS
    at_slot = rows((wide, SLOTS)) // FLUX == lanes((wide, SLOTS))
    at_group = rows((wide, GROUPS)) // (FLUX * CAP) == lanes((wide, GROUPS))
    source = jnp.where(at_slot, source_v[...].astype(F32), 0.0).astype(BF16)
    count = jnp.where(at_group, count_v[...].astype(F32), 0.0).astype(BF16)
    source = jnp.dot(source, jnp.ones((SLOTS, COLS), BF16), preferred_element_type=F32)
    count = jnp.dot(count, jnp.ones((GROUPS, COLS), BF16), preferred_element_type=F32)
    r, c = rows((wide, COLS)), lanes((wide, COLS))
    pick = (
        (source == (c // FLUX).astype(F32))
        & (r % FLUX == c % FLUX)
        & (((r // FLUX) % CAP).astype(F32) < count)
    )
    chosen = jnp.dot(jnp.where(pick, 1.0, 0.0).astype(BF16), blocks, preferred_element_type=F32)
    low = r % 16 < 8
    lhs_v[:, 0:COLS] = jnp.where(low, chosen, 0.0).astype(BF16)
    lhs_v[:, COLS : 2 * COLS] = jnp.where(low, 0.0, chosen).astype(BF16)

    parts = {}
    for g in range(GROUPS):
        if g != REACH:
            parts[g] = pltpu.make_async_remote_copy(
                src_ref=send_v.at[g], dst_ref=recv_v.at[g], send_sem=part_send.at[g],
                recv_sem=part_recv.at[g], device_id=along(g - REACH), device_id_type=MESH,
            )

    half = rows((16, COLS)) % 8 < 4
    halo = halo_copies(0)
    for i, g in enumerate(ORDER):
        weights[g].wait()
        for q in (2 * g, 2 * g + 1):
            w = [weight_v[4 * q + j] for j in range(4)]
            tile = jnp.concatenate(
                [jnp.concatenate(w[0:2], axis=1), jnp.concatenate(w[2:4], axis=1)], axis=0
            )
            both = jnp.dot(lhs_v[pl.ds(16 * q, 16), :], tile, preferred_element_type=F32)
            value = jnp.where(half, both[:, 0:COLS], both[:, COLS:])
            target = recv_v if g == REACH else send_v
            target[g, pl.ds(16 * (q - 2 * g), 16), :] = value
        if i == 0:
            pl.semaphore_wait(barrier, len(partners))
        if g != REACH:
            parts[g].start()
        if i == 1:
            for copy in halo:
                copy.start()

    loads["place"].wait()
    expand = jnp.where(lanes((SLOTS, wide)) // FLUX == rows((SLOTS, wide)), 1.0, 0.0).astype(BF16)
    target_row = jnp.dot(
        jnp.broadcast_to(place_v[...].astype(F32), (8, SLOTS)).astype(BF16), expand, preferred_element_type=F32
    )
    r, c = rows((FLUX * ROWS, wide)), lanes((FLUX * ROWS, wide))
    place = jnp.where(
        (target_row[0:1] == (r % ROWS).astype(F32)) & (c % FLUX == r // ROWS), 1.0, 0.0
    ).astype(BF16)

    loads["east"].wait()
    loads["north"].wait()

    def edges(e):
        north_rows, south_rows = row_in[e, 0], row_in[e, 1]
        north_rows = jnp.where(oy == n_oy - 1, 0.0, north_rows)
        south_rows = jnp.where(oy == 0, 0.0, south_rows)
        return north_rows, south_rows, col_in[e, 0], col_in[e, 1]

    for copy in halo:
        copy.wait_recv()
    at_east, at_west = lane == COLS - 1, lane == 0
    at_north, at_south = row == ROWS - 1, row == 0

    def sides(x, k, halo_in):
        north_rows, south_rows, west_cols, east_cols = halo_in
        east = jnp.where(at_east, shift(east_cols, COLS - 2 - 2 * k, 1), shift(x, -1, 1))
        west = jnp.where(at_west, shift(west_cols, -2 * k, 1), shift(x, 1, 1))
        north = jnp.where(at_north, north_rows[k : k + 1], shift(x, -1, 0))
        south = jnp.where(at_south, south_rows[k : k + 1], shift(x, 1, 0))
        return east, west, north, south

    halo_in = edges(0)
    wet_east, wet_west, wet_north, wet_south = sides(wet, FIELDS, halo_in)
    coefs = []
    for level in range(LEVELS):
        u, v = east_v[level], north_v[level]
        ce = wet * (LATERAL * wet_east - jnp.minimum(u, 0.0))
        cw = wet * (LATERAL * wet_west + jnp.maximum(u, 0.0))
        cn = wet * (LATERAL * wet_north - jnp.minimum(v, 0.0))
        cs = wet * (LATERAL * wet_south + jnp.maximum(v, 0.0))
        coefs.append((1.0 - (ce + cw + cn + cs), ce, cw, cn, cs))
    mix = VERTICAL * wet

    def lateral(x, level, near):
        c0, ce, cw, cn, cs = coefs[level]
        east, west, north, south = near
        return c0 * x + ce * east + cw * west + cn * north + cs * south

    def slot(level, t):
        return level * TRACERS + t

    upper, lower = [], []
    for t in range(TRACERS):
        x = [first[t * LEVELS + level] for level in range(LEVELS)]
        y = [lateral(x[level], level, sides(x[level], t * LEVELS + level, halo_in)) for level in range(LEVELS)]
        d12, d23 = mix * (x[2] - x[1]), mix * (x[3] - x[2])
        y = [y[0], y[1] + d12, y[2] + d23 - d12, y[3] - d23]
        for level in range(LEVELS):
            state_v[pl.ds(slot(level, t) * ROWS, ROWS), :] = y[level]

    def send_edges(e, level):
        base = level * TRACERS * ROWS
        skip = 0 if level == 0 else -2
        row_out[e, 0, 0:8, :] = state_v[pl.ds(base + skip * ROWS, 8, stride=ROWS), :]
        row_out[e, 1, 0:8, :] = state_v[pl.ds(base + skip * ROWS + ROWS - 1, 8, stride=ROWS), :]
        col_out[e] = pack([state_v[pl.ds(base + k * ROWS, ROWS), :] for k in range(2 * TRACERS)])
        copies = halo_copies(e)
        for copy in copies:
            copy.start()
        return copies

    deep = send_edges(1, 2)

    def placed(groups):
        total = None
        for g in groups:
            got = recv_v[g]
            high = got.astype(BF16)
            rest = (got - high.astype(F32)).astype(BF16)
            lhs = place[:, g * CAP * FLUX : (g + 1) * CAP * FLUX]
            term = jnp.dot(lhs, high, preferred_element_type=F32) + jnp.dot(lhs, rest, preferred_element_type=F32)
            total = term if total is None else total + term
        return total

    for g in NEAR:
        if g != REACH:
            parts[g].wait_recv()
    ocean = placed(NEAR)
    for g in FAR:
        parts[g].wait_recv()
    ocean = ocean + placed(FAR)
    ocean_o[...] = ocean
    q = ocean[(FLUX - 1) * ROWS :]
    top = wet * (0.05 + 0.15 * q * q / (1.0 + q * q))
    surface = [GAIN * wet * ocean[t * ROWS : (t + 1) * ROWS] for t in range(TRACERS)]

    for t in range(TRACERS):
        d01 = top * (first[t * LEVELS + 1] - first[t * LEVELS])
        for level, change in ((0, d01 + surface[t]), (1, -d01)):
            where = pl.ds(slot(level, t) * ROWS, ROWS)
            state_v[where, :] = state_v[where, :] + change
    shallow = send_edges(2, 0)

    for copy in deep:
        copy.wait_recv()
    halo_in = edges(1)
    state = [[state_v[pl.ds(slot(level, t) * ROWS, ROWS), :] for level in range(LEVELS)] for t in range(TRACERS)]
    skip = 2 * TRACERS
    for t in range(TRACERS):
        x = state[t]
        d12, d23 = mix * (x[2] - x[1]), mix * (x[3] - x[2])
        for level, change in ((2, d23 - d12), (3, -d23)):
            k = slot(level, t) - skip
            north_rows, south_rows, west_cols, east_cols = halo_in
            near = sides(x[level], k, (north_rows[2:8], south_rows[2:8], west_cols, east_cols))
            new_o[pl.ds((t * LEVELS + level) * ROWS, ROWS), :] = lateral(x[level], level, near) + change
    for copy in shallow:
        copy.wait_recv()
    halo_in = edges(2)
    for t in range(TRACERS):
        x = state[t]
        d01, d12 = top * (x[1] - x[0]), mix * (x[2] - x[1])
        for level, change in ((0, d01 + surface[t]), (1, d12 - d01)):
            near = sides(x[level], slot(level, t), halo_in)
            new_o[pl.ds((t * LEVELS + level) * ROWS, ROWS), :] = lateral(x[level], level, near) + change

    for g in parts:
        parts[g].wait_send()
    for copy in halo + deep + shallow:
        copy.wait_send()


def body(
    atm_flux, remap_weight, source_block, send_counts, recv_rows, land_mask, tracers, east_velocity, north_velocity
):
    hbm = pl.BlockSpec(memory_space=pltpu.HBM)
    vmem = pl.BlockSpec(memory_space=pltpu.VMEM)
    ocean, new = pl.pallas_call(
        kernel,
        out_shape=(
            jax.ShapeDtypeStruct((FLUX * ROWS, COLS), F32),
            jax.ShapeDtypeStruct((FIELDS * ROWS, COLS), F32),
        ),
        in_specs=[hbm] * 9,
        out_specs=(vmem, vmem),
        scratch_shapes=[
            pltpu.VMEM((FLUX, BLOCKS * COLS), BF16),
            pltpu.VMEM((SLOTS, COLS, COLS), BF16),
            pltpu.VMEM((1, SLOTS), jnp.int32),
            pltpu.VMEM((1, GROUPS), jnp.int32),
            pltpu.VMEM((1, SLOTS), jnp.int32),
            pltpu.VMEM((ROWS, COLS), jnp.int32),
            pltpu.VMEM((FIELDS * ROWS, COLS), F32),
            pltpu.VMEM((LEVELS, ROWS, COLS), F32),
            pltpu.VMEM((LEVELS, ROWS, COLS), F32),
            pltpu.VMEM((FLUX * SLOTS, 2 * COLS), BF16),
            pltpu.VMEM((GROUPS, FLUX * CAP, COLS), F32),
            pltpu.VMEM((GROUPS, FLUX * CAP, COLS), F32),
            pltpu.VMEM((FIELDS * ROWS, COLS), F32),
            pltpu.VMEM((3, ROWS, COLS), F32),
            pltpu.VMEM((3, 2, ROWS, COLS), F32),
            pltpu.VMEM((3, 2, ROWS, COLS), F32),
            pltpu.VMEM((3, 2, ROWS, COLS), F32),
            pltpu.SemaphoreType.DMA((8,)),
            pltpu.SemaphoreType.DMA((GROUPS,)),
            pltpu.SemaphoreType.DMA((GROUPS,)),
            pltpu.SemaphoreType.DMA((GROUPS,)),
            pltpu.SemaphoreType.DMA((3, 4)),
            pltpu.SemaphoreType.DMA((3, 4)),
        ],
        compiler_params=pltpu.CompilerParams(
            collective_id=0, has_side_effects=True, vmem_limit_bytes=32 * 1024 * 1024
        ),
    )(*(pltpu.with_memory_space_constraint(a, pltpu.HBM) for a in (
        atm_flux.reshape(FLUX, BLOCKS * COLS),
        remap_weight.reshape(SLOTS, COLS, COLS),
        source_block,
        send_counts,
        recv_rows,
        land_mask,
        tracers.reshape(FIELDS * ROWS, COLS),
        east_velocity,
        north_velocity,
    )))
    return (ocean.reshape(FLUX, ROWS, COLS), new.reshape(TRACERS, LEVELS, ROWS, COLS))


def solution(mesh):
    in_specs = (
        P(None, "oy", "ox"),
        P("oy", "ox", None, None),
        P("oy", "ox"),
        P("oy", "ox"),
        P("oy", "ox"),
        P("oy", "ox"),
        P(None, None, "oy", "ox"),
        P(None, "oy", "ox"),
        P(None, "oy", "ox"),
    )
    out_specs = (P(None, "oy", "ox"), P(None, None, "oy", "ox"))
    return jax.shard_map(body, mesh=mesh, in_specs=in_specs, out_specs=out_specs, check_vma=False)
```

time: 85.3 us -> 32 us (0.38)
  the two profiles are of different devices: /device:TPU:57 before, /device:TPU:96 now
where the time goes in v1:
time: 32 us; the launch traced here: 31.8 us
  Pallas kernels  29.9 us (93%)
  local copies, waits for them, and re-layouts  1.26 us (4%)
  between operations  0.64 us (2%)
    pallas_call x1, Pallas kernels, body(): pl.pallas_call(kernel, out_shape=(jax.ShapeDtypeStruct((FLUX * ROWS, COLS...  29.9 us
    unnamed x2, local copies, waits for them, and re-layouts  1.26 us

profile of v1, /device:TPU:96, one launch (start us, length us, event | category | flops | bytes accessed | tf_op | source)
XLA Modules:
  0.0 31.8 jit_solution(8292268721950882969)
XLA Ops:
  0.6 29.9 %shard_map.104 = (f32[64,128]{1,0:T(8,128)S(1)}, f32[192,128]{1,0:T(8,128)S(1)}) custom-call(bf16[4,768]{1,0:T(4,128)(2,1)} %bitcast.9, bf16[56,128,128]{2,1,0:T(8,128)(2,1)} %bitcast.7, s32[1,56]{1,0:T(1,128)} %source_h.1, s32[1,7]{1,0:T(1,128)} %count_h.1, s32[1,56]{1,0:T(1,128)} %recv_h.1, s32[16,128]{1,0:T(8,128)} %land_h.1, f32[192,128]{1,0:T(8,128)} %bitcast.8, ...), custom_call_target="tpu_custom_call" | custom-call | tf_op jit(solution)/shard_map/pallas_call | solution.py:304
  30.5 0.6 %copy.13 = f32[4,16,128]{2,1,0:T(8,128)} copy(f32[4,16,128]{2,1,0:T(8,128)S(1)} %bitcast.6) | data formatting | bytes 65536
  31.2 0.6 %copy.14 = f32[3,4,16,128]{3,2,1,0:T(8,128)} copy(f32[3,4,16,128]{3,2,1,0:T(8,128)S(1)} %bitcast.5) | data formatting | bytes 196608

commit v2 on v1

v2 whole, which is shorter than its diff:
```python
import jax
import jax.numpy as jnp
from jax import lax
from jax.experimental import pallas as pl
from jax.experimental.pallas import tpu as pltpu
from jax.sharding import PartitionSpec as P

MESH = pl.DeviceIdType.MESH
FLUX = 4
TRACERS = 3
LEVELS = 4
FIELDS = TRACERS * LEVELS
ROWS = 16
COLS = 128
BLOCKS = 6
REACH = 3
CAP = 8
GROUPS = 7
SLOTS = GROUPS * CAP
RING = 8
SPAN = REACH + 1
OFFSETS = (-4, -3, -2, -1, 1, 2, 3, 4)
SENDS = (1, 2, 3, 4, -4, -3, -2, -1)
DATA = 32
AHEAD = (6, 5, 4, 3)
BEHIND = (0, 1, 2)
EAST_AT = 16
NORTH_AT = 20
LATERAL = 0.08
VERTICAL = 0.1
GAIN = 0.5
F32 = jnp.float32
BF16 = jnp.bfloat16


def lanes(shape):
    return lax.broadcasted_iota(jnp.int32, shape, len(shape) - 1)


def rows(shape):
    return lax.broadcasted_iota(jnp.int32, shape, len(shape) - 2)


def kernel(
    flux_h, weight_h, source_h, count_h, recv_h, land_h, tracer_h, east_h, north_h,
    ocean_o, new_o,
    flux_v, weight_v, source_v, count_v, place_v, land_v, tracer_v, east_v, north_v,
    lhs_v, part_v, edge_v, send_v, recv_v, state_v, col_out, col_in, row_out, row_in,
    load_sem, weight_sem, part_send, part_recv, halo_send, halo_recv, ack_sem,
):
    oy, ox = lax.axis_index("oy"), lax.axis_index("ox")
    n_oy, n_ox = lax.axis_size("oy"), lax.axis_size("ox")

    def along(offset):
        return (oy, lax.rem(ox + (n_ox + offset), n_ox))

    up = (lax.rem(oy + 1, n_oy), ox)
    down = (lax.rem(oy + (n_oy - 1), n_oy), ox)

    loads = {}
    for i, (name, src, dst) in enumerate((
        ("tracer", tracer_h, tracer_v), ("land", land_h, land_v), ("flux", flux_h, flux_v),
        ("source", source_h, source_v), ("count", count_h, count_v), ("place", recv_h, place_v),
        ("east", east_h, east_v), ("north", north_h, north_v),
    )):
        loads[name] = pltpu.make_async_copy(src, dst, load_sem.at[i])
    weights = {
        g: pltpu.make_async_copy(
            weight_h.at[pl.ds(g * CAP, CAP)], weight_v.at[pl.ds(g * CAP, CAP)], weight_sem.at[g]
        )
        for g in range(GROUPS)
    }
    for name in ("flux", "source", "count", "tracer", "land", "place", "east", "north"):
        loads[name].start()
    for g in AHEAD + BEHIND:
        weights[g].start()

    key = lax.rem(ox, RING)
    odd = lax.rem(oy, 2)
    partners = {d: along(d) for d in OFFSETS}
    partners["up"], partners["down"] = up, down
    later = {d: lax.rem(key + (d + RING), RING) > key for d in OFFSETS}
    later["up"] = (odd == 1) & (oy != n_oy - 1)
    later["down"] = (odd == 1) | (oy == 0)
    opposite = {d: -d for d in OFFSETS} | {"up": "down", "down": "up"}
    place_of = {d: i for i, d in enumerate(partners)}
    barrier = pltpu.get_barrier_semaphore()
    announced = jnp.int32(0)
    for d in partners:
        announced += jnp.where(later[d], 0, 1)

        @pl.when(later[d])
        def _():
            pl.semaphore_signal(barrier, inc=1, device_id=partners[d], device_id_type=MESH)

    def remote(src, dst, send, recv, device):
        return pltpu.make_async_remote_copy(
            src_ref=src, dst_ref=dst, send_sem=send, recv_sem=recv, device_id=device, device_id_type=MESH
        )

    def row_copies(e):
        return {
            "down": remote(row_out.at[e, 0], row_in.at[e, 0], halo_send.at[e, 0], halo_recv.at[e, 0], down),
            "up": remote(row_out.at[e, 1], row_in.at[e, 1], halo_send.at[e, 1], halo_recv.at[e, 1], up),
        }

    first_rows = row_copies(0)
    columns = {
        1: remote(col_out.at[0], col_in.at[0], halo_send.at[2, 0], halo_recv.at[2, 0], partners[1]),
        -1: remote(col_out.at[1], col_in.at[1], halo_send.at[2, 1], halo_recv.at[2, 1], partners[-1]),
    }
    parts = {}
    for d in OFFSETS:
        if abs(d) <= REACH:
            src, dst = send_v.at[d + REACH], recv_v.at[d + SPAN]
        else:
            src, dst = edge_v.at[int(d > 0)], recv_v.at[d + SPAN, pl.ds(DATA, 8)]
        parts[d] = remote(src, dst, part_send.at[d + SPAN], part_recv.at[d + SPAN], partners[d])

    lane = lanes((ROWS, COLS))
    row = rows((ROWS, COLS))

    def shift(x, by, axis):
        return pltpu.roll(x, by % x.shape[axis], axis)

    for name in ("flux", "source", "count", "tracer", "land", "place", "east", "north"):
        loads[name].wait()
    flux = flux_v[...].astype(F32)
    blocks = jnp.concatenate([flux[:, n * COLS : (n + 1) * COLS] for n in range(BLOCKS)], axis=0)
    blocks = jnp.concatenate([blocks, jnp.zeros((COLS - FLUX * BLOCKS, COLS), F32)], axis=0).astype(BF16)
    wide = FLUX * SLOTS
    at_slot = rows((wide, SLOTS)) // FLUX == lanes((wide, SLOTS))
    at_group = rows((wide, GROUPS)) // DATA == lanes((wide, GROUPS))
    source = jnp.where(at_slot, source_v[...].astype(F32), 0.0).astype(BF16)
    count = jnp.where(at_group, count_v[...].astype(F32), 0.0).astype(BF16)
    source = jnp.dot(source, jnp.ones((SLOTS, COLS), BF16), preferred_element_type=F32)
    count = jnp.dot(count, jnp.ones((GROUPS, COLS), BF16), preferred_element_type=F32)
    r, c = rows((wide, COLS)), lanes((wide, COLS))
    pick = (
        (source == (c // FLUX).astype(F32))
        & (r % FLUX == c % FLUX)
        & (((r // FLUX) % CAP).astype(F32) < count)
    )
    chosen = jnp.dot(jnp.where(pick, 1.0, 0.0).astype(BF16), blocks, preferred_element_type=F32)
    low = r % 16 < 8
    lhs_v[:, 0:COLS] = jnp.where(low, chosen, 0.0).astype(BF16)
    lhs_v[:, COLS : 2 * COLS] = jnp.where(low, 0.0, chosen).astype(BF16)

    wet = land_v[...].astype(F32)
    first = [tracer_v[pl.ds(k * ROWS, ROWS), :] for k in range(FIELDS)]
    for side, at in ((0, 0), (1, ROWS - 1)):
        row_out[0, side, 0:FIELDS, :] = tracer_v[pl.ds(at, FIELDS, stride=ROWS), :]
        row_out[0, side, FIELDS:ROWS, :] = jnp.broadcast_to(wet[at : at + 1], (ROWS - FIELDS, COLS))
    packed = {k: first[k] for k in range(FIELDS)} | {FIELDS: wet}
    packed |= {EAST_AT + k: east_v[k] for k in range(LEVELS)} | {NORTH_AT + k: north_v[k] for k in range(LEVELS)}
    to_east = jnp.zeros((ROWS, COLS), F32)
    to_west = jnp.zeros((ROWS, COLS), F32)
    for k, field in packed.items():
        to_east = jnp.where(lane // 2 == k, shift(field, 2 * k + 2, 1), to_east)
        to_west = jnp.where(lane // 2 == k, shift(field, 2 * k, 1), to_west)
    margin = jnp.broadcast_to(place_v[...].astype(F32), (8, SLOTS)).astype(BF16)
    same = jnp.where(lanes((SLOTS, COLS)) == rows((SLOTS, COLS)), 1.0, 0.0).astype(BF16)
    margin = jnp.dot(margin, same, preferred_element_type=F32)
    for i, value in enumerate((to_east, to_west)):
        col_out[i, 0:ROWS, :] = value
        col_out[i, ROWS:, :] = margin

    half = rows((16, COLS)) % 8 < 4
    edge_row = rows((8, COLS))
    ends = jnp.where(lanes((8, COLS)) == jnp.where(edge_row < 2, 0, COLS - 1), 1.0, 0.0).astype(BF16)
    dims = (((1,), (1,)), ((), ()))

    def split(x):
        high = x.astype(BF16)
        return high, (x - high.astype(F32)).astype(BF16)

    def remap(groups):
        for g in groups:
            weights[g].wait()
        for g in groups:
            for q in (2 * g, 2 * g + 1):
                w = [weight_v[4 * q + j] for j in range(4)]
                tile = jnp.concatenate(
                    [jnp.concatenate(w[0:2], axis=1), jnp.concatenate(w[2:4], axis=1)], axis=0
                )
                both = jnp.dot(lhs_v[pl.ds(16 * q, 16), :], tile, preferred_element_type=F32)
                value = jnp.where(half, both[:, 0:COLS], both[:, COLS:])
                part_v[pl.ds(16 * q, 16), :] = value
                if g == REACH:
                    recv_v[SPAN, pl.ds(16 * (q - 2 * g), 16), :] = value
                else:
                    send_v[g, pl.ds(16 * (q - 2 * g), 16), :] = value

    def edge_columns(base, groups, at):
        high, rest = split(part_v[pl.ds(base * DATA, COLS), :])
        edge = lax.dot_general(ends, high, dims, preferred_element_type=F32)
        edge = edge + lax.dot_general(ends, rest, dims, preferred_element_type=F32)
        for g in groups:
            send_v[g, DATA:, :] = edge
        edge_v[at] = edge

    remap(AHEAD)
    edge_columns(REACH, AHEAD[:-1], 1)

    @pl.when(announced > 0)
    def _():
        pl.semaphore_wait(barrier, announced)

    for d in partners:
        @pl.when(jnp.logical_not(later[d]))
        def _():
            pl.semaphore_signal(
                ack_sem.at[place_of[opposite[d]]], inc=1, device_id=partners[d], device_id_type=MESH
            )

    @pl.when(jnp.logical_not(later[1]))
    def _():
        columns[1].start()
    for d in SENDS[0:SPAN]:
        @pl.when(jnp.logical_not(later[d]))
        def _():
            parts[d].start()

    remap(BEHIND)
    edge_columns(0, BEHIND, 0)

    for d in SENDS[SPAN:]:
        @pl.when(jnp.logical_not(later[d]))
        def _():
            parts[d].start()
    for d, copy in (("up", first_rows["up"]), ("down", first_rows["down"]), (-1, columns[-1])):
        @pl.when(jnp.logical_not(later[d]))
        def _():
            copy.start()
    for d in ("up", "down"):
        @pl.when(later[d])
        def _():
            pl.semaphore_wait(ack_sem.at[place_of[d]], 1)
            first_rows[d].start()
    for d in SENDS:
        @pl.when(later[d])
        def _():
            pl.semaphore_wait(ack_sem.at[place_of[d]], 1)
            if d in columns:
                columns[d].start()
            parts[d].start()

    def edges(e):
        north_rows, south_rows = row_in[e, 0], row_in[e, 1]
        north_rows = jnp.where(oy == n_oy - 1, 0.0, north_rows)
        south_rows = jnp.where(oy == 0, 0.0, south_rows)
        return north_rows, south_rows

    for copy in (*first_rows.values(), *columns.values()):
        copy.wait_recv()
    at_east, at_west = lane == COLS - 1, lane == 0
    at_north, at_south = row == ROWS - 1, row == 0
    north_rows, south_rows = edges(0)
    from_west, from_east = col_in[0, 0:ROWS], col_in[1, 0:ROWS]

    def to_edge(x, k, side):
        return shift(x, COLS - 1 - 2 * k, 1) if side == "east" else shift(x, -2 * k - 1, 1)

    def sides(x, k):
        east = jnp.where(at_east, to_edge(from_east, k, "east"), shift(x, -1, 1))
        west = jnp.where(at_west, to_edge(from_west, k, "west"), shift(x, 1, 1))
        north = jnp.where(at_north, north_rows[k : k + 1], shift(x, -1, 0))
        south = jnp.where(at_south, south_rows[k : k + 1], shift(x, 1, 0))
        return east, west, north, south

    wet_east, wet_west, wet_north, wet_south = sides(wet, FIELDS)
    coefs = []
    for level in range(LEVELS):
        u, v = east_v[level], north_v[level]
        ce = wet * (LATERAL * wet_east - jnp.minimum(u, 0.0))
        cw = wet * (LATERAL * wet_west + jnp.maximum(u, 0.0))
        cn = wet * (LATERAL * wet_north - jnp.minimum(v, 0.0))
        cs = wet * (LATERAL * wet_south + jnp.maximum(v, 0.0))
        coefs.append((1.0 - (ce + cw + cn + cs), ce, cw, cn, cs))
    mix = VERTICAL * wet

    def lateral(x, level, near):
        c0, ce, cw, cn, cs = coefs[level]
        east, west, north, south = near
        return c0 * x + ce * east + cw * west + cn * north + cs * south

    for t in range(TRACERS):
        x = first[t * LEVELS : (t + 1) * LEVELS]
        y = [lateral(x[level], level, sides(x[level], t * LEVELS + level)) for level in range(LEVELS)]
        d12, d23 = mix * (x[2] - x[1]), mix * (x[3] - x[2])
        for level, value in enumerate((y[0], y[1] + d12, y[2] + d23 - d12, y[3] - d23)):
            state_v[pl.ds((t * LEVELS + level) * ROWS, ROWS), :] = value

    lists = jnp.where(edge_row == 0, margin, jnp.where(edge_row == 1, col_in[0, ROWS:], col_in[1, ROWS:]))
    c = lanes((COLS, 2 * COLS))
    slot_at = jnp.where(c < COLS, c // FLUX, (c - COLS) // FLUX + REACH * CAP)
    expand = jnp.where(slot_at == rows((COLS, 2 * COLS)), 1.0, 0.0).astype(BF16)
    target_row = jnp.dot(lists.astype(BF16), expand, preferred_element_type=F32)
    r, c = rows((FLUX * ROWS, 2 * COLS)), lanes((FLUX * ROWS, 2 * COLS))
    place = jnp.where(
        (target_row[0:1] == (r % ROWS).astype(F32)) & (c % FLUX == r // ROWS), 1.0, 0.0
    ).astype(BF16)
    r = rows((ROWS, 2 * COLS)).astype(F32)
    on_row = [target_row[i : i + 1] == r for i in (1, 2)]
    c = lanes((2 * COLS, 2 * COLS))
    gather = jnp.where(
        rows((2 * COLS, 2 * COLS)) % FLUX == jnp.where(c < COLS, FLUX - 1, (c - COLS) // (2 * LEVELS)), 1.0, 0.0
    ).astype(BF16)

    level_of = (lane // 2) % LEVELS

    def beside(i):
        if i == 0:
            x, own, way, own_wet = from_west, to_west, 1, to_west[:, 2 * FIELDS : 2 * FIELDS + 1]
        else:
            x, own, way, own_wet = from_east, to_east, -1, to_east[:, 2 * FIELDS + 1 : 2 * FIELDS + 2]
        center = 2 * FIELDS + (1 - i)
        wet_c = jnp.broadcast_to(x[:, center : center + 1], (ROWS, COLS))
        wet_far = jnp.broadcast_to(x[:, center - way : center - way + 1], (ROWS, COLS))
        wet_own = jnp.broadcast_to(own_wet, (ROWS, COLS))

        def spread(at):
            moved = [shift(x, 2 * (t * LEVELS - at), 1) for t in range(TRACERS)]
            return jnp.where(lane < 2 * LEVELS, moved[0], jnp.where(lane < 4 * LEVELS, moved[1], moved[2]))

        u, v = spread(EAST_AT), spread(NORTH_AT)
        far, own = shift(x, way, 1), shift(own, way, 1)
        plus, minus = jnp.maximum(u, 0.0), -jnp.minimum(u, 0.0)
        c_far, c_own = (plus, minus) if i == 0 else (minus, plus)
        change = (LATERAL * wet_far + c_far) * (far - x) + (LATERAL * wet_own + c_own) * (own - x)
        step = shift(x, -2, 1) - x
        return x, wet_c, v, change, step

    halves = [beside(0), beside(1)]

    for d in OFFSETS:
        parts[d].wait_recv()
    arrived = [recv_v[g - REACH + SPAN, 0:DATA] for g in range(GROUPS)]
    arrived = jnp.concatenate(arrived[:SPAN] + [jnp.zeros((DATA, COLS), F32)] + arrived[SPAN:], axis=0)
    high, rest = split(arrived)
    ocean = jnp.dot(place, high, preferred_element_type=F32) + jnp.dot(place, rest, preferred_element_type=F32)
    ocean_o[...] = ocean
    q = ocean[(FLUX - 1) * ROWS :]
    top = wet * (0.05 + 0.15 * q * q / (1.0 + q * q))
    surface = [GAIN * wet * ocean[t * ROWS : (t + 1) * ROWS] for t in range(TRACERS)]
    for t in range(TRACERS):
        d01 = top * (first[t * LEVELS + 1] - first[t * LEVELS])
        for level, change in ((0, d01 + surface[t]), (1, -d01)):
            where = pl.ds((t * LEVELS + level) * ROWS, ROWS)
            state_v[where, :] = state_v[where, :] + change

    for side, at in ((0, 0), (1, ROWS - 1)):
        row_out[1, side, 0:FIELDS, :] = state_v[pl.ds(at, FIELDS, stride=ROWS), :]
        row_out[1, side, FIELDS : FIELDS + 1, :] = from_west[at : at + 1]
        row_out[1, side, FIELDS + 1 : FIELDS + 2, :] = from_east[at : at + 1]
        row_out[1, side, FIELDS + 2 :, :] = jnp.zeros((2, COLS), F32)
    second_rows = row_copies(1)
    for copy in second_rows.values():
        copy.start()

    quarter = lanes((8, COLS)) // DATA

    def along_lanes(base, at):
        out = [jnp.zeros((8, COLS), F32)] * 2
        for g in range(GROUPS):
            d = base + g
            ahead = d > 0 or (d == 0 and base != -2)
            value = recv_v[d + SPAN, DATA:] if d != 0 else edge_v[int(ahead)]
            out[ahead] = jnp.where(quarter == (g - REACH if ahead else g), value, out[ahead])
        return jnp.concatenate([tile[at : at + 1] for tile in out], axis=1)

    terms = [
        jnp.where(on_row[0], along_lanes(-2, 2), 0.0),
        jnp.where(on_row[1], along_lanes(-4, 0), 0.0),
    ]
    high, rest = split(jnp.concatenate(terms, axis=0))
    margins = jnp.dot(high, gather, preferred_element_type=F32) + jnp.dot(rest, gather, preferred_element_type=F32)
    inner = []
    for i, (x, wet_c, v, change, step) in enumerate(halves):
        q = margins[i * ROWS : (i + 1) * ROWS, 0:COLS]
        kv = 0.05 + 0.15 * q * q / (1.0 + q * q)
        face = jnp.where(level_of == LEVELS - 1, 0.0, jnp.where(level_of == 0, kv, VERTICAL) * step)
        source = jnp.where(level_of == 0, GAIN * margins[i * ROWS : (i + 1) * ROWS, COLS:], shift(-face, 2, 1))
        inner.append(change + face + source)

    for t in range(TRACERS):
        x = [state_v[pl.ds((t * LEVELS + level) * ROWS, ROWS), :] for level in range(LEVELS)]
        d01, d12, d23 = top * (x[1] - x[0]), mix * (x[2] - x[1]), mix * (x[3] - x[2])
        changes = (d01 + surface[t], d12 - d01, d23 - d12, -d23)
        for level, change in enumerate(changes):
            y = x[level]
            near = (
                jnp.where(at_east, 0.0, shift(y, -1, 1)),
                jnp.where(at_west, 0.0, shift(y, 1, 1)),
                jnp.where(at_north, 0.0, shift(y, -1, 0)),
                jnp.where(at_south, 0.0, shift(y, 1, 0)),
            )
            new_o[pl.ds((t * LEVELS + level) * ROWS, ROWS), :] = lateral(y, level, near) + change

    for copy in second_rows.values():
        copy.wait_recv()
    north_rows, south_rows = edges(1)
    halo = []
    for i, ((x, wet_c, v, _, _), change) in enumerate(zip(halves, inner)):
        north = jnp.where(at_north, north_rows[FIELDS + i : FIELDS + i + 1], shift(x, -1, 0))
        south = jnp.where(at_south, south_rows[FIELDS + i : FIELDS + i + 1], shift(x, 1, 0))
        center = 2 * FIELDS + (1 - i)
        wet_n = jnp.broadcast_to(north[:, center : center + 1], (ROWS, COLS))
        wet_s = jnp.broadcast_to(south[:, center : center + 1], (ROWS, COLS))
        change = change + (LATERAL * wet_n - jnp.minimum(v, 0.0)) * (north - x)
        change = change + (LATERAL * wet_s + jnp.maximum(v, 0.0)) * (south - x)
        halo.append(x + wet_c * change)
    for level in range(LEVELS):
        _, ce, cw, cn, cs = coefs[level]
        ce, cw = jnp.where(at_east, ce, 0.0), jnp.where(at_west, cw, 0.0)
        cn, cs = jnp.where(at_north, cn, 0.0), jnp.where(at_south, cs, 0.0)
        for t in range(TRACERS):
            k = t * LEVELS + level
            where = pl.ds(k * ROWS, ROWS)
            new_o[where, :] = (
                new_o[where, :]
                + cw * to_edge(halo[0], k, "west")
                + ce * to_edge(halo[1], k, "east")
                + cn * north_rows[k : k + 1]
                + cs * south_rows[k : k + 1]
            )

    for copy in (*parts.values(), *first_rows.values(), *columns.values(), *second_rows.values()):
        copy.wait_send()


def store(ocean_v, new_v, ocean_o, new_o, sem):
    copies = [
        pltpu.make_async_copy(new_v, new_o, sem.at[0]),
        pltpu.make_async_copy(ocean_v, ocean_o, sem.at[1]),
    ]
    for copy in copies:
        copy.start()
    for copy in copies:
        copy.wait()


def body(
    atm_flux, remap_weight, source_block, send_counts, recv_rows, land_mask, tracers, east_velocity, north_velocity
):
    hbm = pl.BlockSpec(memory_space=pltpu.HBM)
    vmem = pl.BlockSpec(memory_space=pltpu.VMEM)
    ocean, new = pl.pallas_call(
        kernel,
        out_shape=(
            jax.ShapeDtypeStruct((FLUX * ROWS, COLS), F32),
            jax.ShapeDtypeStruct((FIELDS * ROWS, COLS), F32),
        ),
        in_specs=[hbm] * 9,
        out_specs=(vmem, vmem),
        scratch_shapes=[
            pltpu.VMEM((FLUX, BLOCKS * COLS), BF16),
            pltpu.VMEM((SLOTS, COLS, COLS), BF16),
            pltpu.VMEM((1, SLOTS), jnp.int32),
            pltpu.VMEM((1, GROUPS), jnp.int32),
            pltpu.VMEM((1, SLOTS), jnp.int32),
            pltpu.VMEM((ROWS, COLS), jnp.int32),
            pltpu.VMEM((FIELDS * ROWS, COLS), F32),
            pltpu.VMEM((LEVELS, ROWS, COLS), F32),
            pltpu.VMEM((LEVELS, ROWS, COLS), F32),
            pltpu.VMEM((FLUX * SLOTS, 2 * COLS), BF16),
            pltpu.VMEM((FLUX * SLOTS, COLS), F32),
            pltpu.VMEM((2, 8, COLS), F32),
            pltpu.VMEM((GROUPS, DATA + 8, COLS), F32),
            pltpu.VMEM((2 * SPAN + 1, DATA + 8, COLS), F32),
            pltpu.VMEM((FIELDS * ROWS, COLS), F32),
            pltpu.VMEM((2, ROWS + 8, COLS), F32),
            pltpu.VMEM((2, ROWS + 8, COLS), F32),
            pltpu.VMEM((2, 2, ROWS, COLS), F32),
            pltpu.VMEM((2, 2, ROWS, COLS), F32),
            pltpu.SemaphoreType.DMA((8,)),
            pltpu.SemaphoreType.DMA((GROUPS,)),
            pltpu.SemaphoreType.DMA((2 * SPAN + 1,)),
            pltpu.SemaphoreType.DMA((2 * SPAN + 1,)),
            pltpu.SemaphoreType.DMA((3, 2)),
            pltpu.SemaphoreType.DMA((3, 2)),
            pltpu.SemaphoreType.REGULAR((len(OFFSETS) + 2,)),
        ],
        compiler_params=pltpu.CompilerParams(
            collective_id=0, has_side_effects=True, vmem_limit_bytes=32 * 1024 * 1024
        ),
    )(*(pltpu.with_memory_space_constraint(a, pltpu.HBM) for a in (
        atm_flux.reshape(FLUX, BLOCKS * COLS),
        remap_weight.reshape(SLOTS, COLS, COLS),
        source_block,
        send_counts,
        recv_rows,
        land_mask,
        tracers.reshape(FIELDS * ROWS, COLS),
        east_velocity,
        north_velocity,
    )))
    ocean, new = pl.pallas_call(
        store,
        out_shape=(
            jax.ShapeDtypeStruct((FLUX * ROWS, COLS), F32),
            jax.ShapeDtypeStruct((FIELDS * ROWS, COLS), F32),
        ),
        in_specs=[vmem, vmem],
        out_specs=(hbm, hbm),
        scratch_shapes=[pltpu.SemaphoreType.DMA((2,))],
    )(*(pltpu.with_memory_space_constraint(a, pltpu.VMEM) for a in (ocean, new)))
    return (ocean.reshape(FLUX, ROWS, COLS), new.reshape(TRACERS, LEVELS, ROWS, COLS))


def solution(mesh):
    in_specs = (
        P(None, "oy", "ox"),
        P("oy", "ox", None, None),
        P("oy", "ox"),
        P("oy", "ox"),
        P("oy", "ox"),
        P("oy", "ox"),
        P(None, None, "oy", "ox"),
        P(None, "oy", "ox"),
        P(None, "oy", "ox"),
    )
    out_specs = (P(None, "oy", "ox"), P(None, None, "oy", "ox"))
    return jax.shard_map(body, mesh=mesh, in_specs=in_specs, out_specs=out_specs, check_vma=False)
```

time: 32 us -> 29.7 us (0.928)
  the two profiles are of different devices: /device:TPU:96 before, /device:TPU:49 now
where the time goes in v2:
time: 29.7 us; the launch traced here: 29.6 us
  Pallas kernels  28.9 us (97%)
  between operations  0.64 us (2%)
    pallas_call x1, Pallas kernels, body(): pl.pallas_call(kernel, out_shape=(jax.ShapeDtypeStruct((FLUX * ROWS, COLS...  28.3 us
    pallas_call x1, Pallas kernels, body(): pl.pallas_call(store, out_shape=(jax.ShapeDtypeStruct((FLUX * ROWS, COLS)...  0.67 us

profile of v2, /device:TPU:49, one launch (start us, length us, event | category | flops | bytes accessed | tf_op | source)
XLA Modules:
  0.0 29.6 jit_solution(13204091231985636169)
XLA Ops:
  0.6 28.3 %shard_map.104 = (f32[64,128]{1,0:T(8,128)S(1)}, f32[192,128]{1,0:T(8,128)S(1)}) custom-call(bf16[4,768]{1,0:T(4,128)(2,1)} %bitcast.7, bf16[56,128,128]{2,1,0:T(8,128)(2,1)} %bitcast.5, s32[1,56]{1,0:T(1,128)} %source_h.1, s32[1,7]{1,0:T(1,128)} %count_h.1, s32[1,56]{1,0:T(1,128)} %recv_h.1, s32[16,128]{1,0:T(8,128)} %land_h.1, f32[192,128]{1,0:T(8,128)} %bitcast.6, ...), custom_call_target="tpu_custom_call" | custom-call | tf_op jit(solution)/shard_map/pallas_call | solution.py:448
  28.9 0.7 %shard_map.105 = (f32[64,128]{1,0:T(8,128)}, f32[192,128]{1,0:T(8,128)}) custom-call(f32[64,128]{1,0:T(8,128)S(1)} %get-tuple-element.6.ocean_v, f32[192,128]{1,0:T(8,128)S(1)} %get-tuple-element.7.new_v), custom_call_target="tpu_custom_call" | custom-call | tf_op jit(solution)/shard_map/pallas_call | solution.py:498

commit v3 on v2

--- a/solution.py
+++ b/solution.py
@@ -64,32 +64,31 @@
         ("east", east_h, east_v), ("north", north_h, north_v),
     )):
         loads[name] = pltpu.make_async_copy(src, dst, load_sem.at[i])
-    weights = {
-        g: pltpu.make_async_copy(
-            weight_h.at[pl.ds(g * CAP, CAP)], weight_v.at[pl.ds(g * CAP, CAP)], weight_sem.at[g]
-        )
-        for g in range(GROUPS)
-    }
+    weights = {}
+    for i, groups in enumerate((AHEAD, BEHIND)):
+        span = pl.ds(min(groups) * CAP, len(groups) * CAP)
+        weights[groups] = pltpu.make_async_copy(weight_h.at[span], weight_v.at[span], weight_sem.at[i])
     for name in ("flux", "source", "count", "tracer", "land", "place", "east", "north"):
         loads[name].start()
-    for g in AHEAD + BEHIND:
-        weights[g].start()
+    for copy in weights.values():
+        copy.start()
 
     key = lax.rem(ox, RING)
     odd = lax.rem(oy, 2)
-    partners = {d: along(d) for d in OFFSETS}
-    partners["up"], partners["down"] = up, down
+    partners = {"up": up, "down": down} | {d: along(d) for d in OFFSETS}
     later = {d: lax.rem(key + (d + RING), RING) > key for d in OFFSETS}
-    later["up"] = (odd == 1) & (oy != n_oy - 1)
-    later["down"] = (odd == 1) | (oy == 0)
+    later["up"] = later["down"] = odd == 1
+    there = {"up": oy != n_oy - 1, "down": oy != 0}
+    late = {d: later[d] & there[d] if d in there else later[d] for d in partners}
+    early = {d: jnp.logical_not(later[d]) & there[d] if d in there else jnp.logical_not(later[d]) for d in partners}
     opposite = {d: -d for d in OFFSETS} | {"up": "down", "down": "up"}
     place_of = {d: i for i, d in enumerate(partners)}
     barrier = pltpu.get_barrier_semaphore()
     announced = jnp.int32(0)
     for d in partners:
-        announced += jnp.where(later[d], 0, 1)
-
-        @pl.when(later[d])
+        announced += jnp.where(early[d], 1, 0)
+
+        @pl.when(late[d])
         def _():
             pl.semaphore_signal(barrier, inc=1, device_id=partners[d], device_id_type=MESH)
 
@@ -175,8 +174,7 @@
         return high, (x - high.astype(F32)).astype(BF16)
 
     def remap(groups):
-        for g in groups:
-            weights[g].wait()
+        weights[groups].wait()
         for g in groups:
             for q in (2 * g, 2 * g + 1):
                 w = [weight_v[4 * q + j] for j in range(4)]
@@ -207,17 +205,17 @@
         pl.semaphore_wait(barrier, announced)
 
     for d in partners:
-        @pl.when(jnp.logical_not(later[d]))
+        @pl.when(early[d])
         def _():
             pl.semaphore_signal(
                 ack_sem.at[place_of[opposite[d]]], inc=1, device_id=partners[d], device_id_type=MESH
             )
 
-    @pl.when(jnp.logical_not(later[1]))
+    @pl.when(early[1])
     def _():
         columns[1].start()
     for d in SENDS[0:SPAN]:
-        @pl.when(jnp.logical_not(later[d]))
+        @pl.when(early[d])
         def _():
             parts[d].start()
 
@@ -225,113 +223,107 @@
     edge_columns(0, BEHIND, 0)
 
     for d in SENDS[SPAN:]:
-        @pl.when(jnp.logical_not(later[d]))
+        @pl.when(early[d])
         def _():
             parts[d].start()
     for d, copy in (("up", first_rows["up"]), ("down", first_rows["down"]), (-1, columns[-1])):
-        @pl.when(jnp.logical_not(later[d]))
+        @pl.when(early[d])
         def _():
             copy.start()
     for d in ("up", "down"):
-        @pl.when(later[d])
+        @pl.when(late[d])
         def _():
             pl.semaphore_wait(ack_sem.at[place_of[d]], 1)
             first_rows[d].start()
-    for d in SENDS:
-        @pl.when(later[d])
-        def _():
-            pl.semaphore_wait(ack_sem.at[place_of[d]], 1)
-            if d in columns:
-                columns[d].start()
-            parts[d].start()
-
     def edges(e):
         north_rows, south_rows = row_in[e, 0], row_in[e, 1]
         north_rows = jnp.where(oy == n_oy - 1, 0.0, north_rows)
         south_rows = jnp.where(oy == 0, 0.0, south_rows)
         return north_rows, south_rows
 
-    for copy in (*first_rows.values(), *columns.values()):
-        copy.wait_recv()
+    def of_rows(copies, wait):
+        for d, copy in copies.items():
+            @pl.when(there[d if wait == "send" else opposite[d]])
+            def _():
+                copy.wait_send() if wait == "send" else copy.wait_recv()
+
+    of_rows(first_rows, "recv")
     at_east, at_west = lane == COLS - 1, lane == 0
     at_north, at_south = row == ROWS - 1, row == 0
     north_rows, south_rows = edges(0)
-    from_west, from_east = col_in[0, 0:ROWS], col_in[1, 0:ROWS]
-
-    def to_edge(x, k, side):
-        return shift(x, COLS - 1 - 2 * k, 1) if side == "east" else shift(x, -2 * k - 1, 1)
-
-    def sides(x, k):
-        east = jnp.where(at_east, to_edge(from_east, k, "east"), shift(x, -1, 1))
-        west = jnp.where(at_west, to_edge(from_west, k, "west"), shift(x, 1, 1))
-        north = jnp.where(at_north, north_rows[k : k + 1], shift(x, -1, 0))
-        south = jnp.where(at_south, south_rows[k : k + 1], shift(x, 1, 0))
-        return east, west, north, south
-
-    wet_east, wet_west, wet_north, wet_south = sides(wet, FIELDS)
+
+    def above(x, k):
+        return jnp.where(at_north, north_rows[k : k + 1], shift(x, -1, 0))
+
+    def below(x, k):
+        return jnp.where(at_south, south_rows[k : k + 1], shift(x, 1, 0))
+
+    wet_east, wet_west = shift(wet, -1, 1), shift(wet, 1, 1)
+    wet_north, wet_south = above(wet, FIELDS), below(wet, FIELDS)
     coefs = []
     for level in range(LEVELS):
         u, v = east_v[level], north_v[level]
-        ce = wet * (LATERAL * wet_east - jnp.minimum(u, 0.0))
-        cw = wet * (LATERAL * wet_west + jnp.maximum(u, 0.0))
+        ce = jnp.where(at_east, 0.0, wet * (LATERAL * wet_east - jnp.minimum(u, 0.0)))
+        cw = jnp.where(at_west, 0.0, wet * (LATERAL * wet_west + jnp.maximum(u, 0.0)))
         cn = wet * (LATERAL * wet_north - jnp.minimum(v, 0.0))
         cs = wet * (LATERAL * wet_south + jnp.maximum(v, 0.0))
         coefs.append((1.0 - (ce + cw + cn + cs), ce, cw, cn, cs))
     mix = VERTICAL * wet
 
-    def lateral(x, level, near):
+    def lateral(x, level, north, south):
         c0, ce, cw, cn, cs = coefs[level]
-        east, west, north, south = near
-        return c0 * x + ce * east + cw * west + cn * north + cs * south
+        return c0 * x + ce * shift(x, -1, 1) + cw * shift(x, 1, 1) + cn * north + cs * south
 
     for t in range(TRACERS):
         x = first[t * LEVELS : (t + 1) * LEVELS]
-        y = [lateral(x[level], level, sides(x[level], t * LEVELS + level)) for level in range(LEVELS)]
+        y = []
+        for level in range(LEVELS):
+            k = t * LEVELS + level
+            y.append(lateral(x[level], level, above(x[level], k), below(x[level], k)))
         d12, d23 = mix * (x[2] - x[1]), mix * (x[3] - x[2])
         for level, value in enumerate((y[0], y[1] + d12, y[2] + d23 - d12, y[3] - d23)):
             state_v[pl.ds((t * LEVELS + level) * ROWS, ROWS), :] = value
 
-    lists = jnp.where(edge_row == 0, margin, jnp.where(edge_row == 1, col_in[0, ROWS:], col_in[1, ROWS:]))
     c = lanes((COLS, 2 * COLS))
     slot_at = jnp.where(c < COLS, c // FLUX, (c - COLS) // FLUX + REACH * CAP)
     expand = jnp.where(slot_at == rows((COLS, 2 * COLS)), 1.0, 0.0).astype(BF16)
-    target_row = jnp.dot(lists.astype(BF16), expand, preferred_element_type=F32)
+    target_row = jnp.dot(margin.astype(BF16), expand, preferred_element_type=F32)
     r, c = rows((FLUX * ROWS, 2 * COLS)), lanes((FLUX * ROWS, 2 * COLS))
     place = jnp.where(
         (target_row[0:1] == (r % ROWS).astype(F32)) & (c % FLUX == r // ROWS), 1.0, 0.0
     ).astype(BF16)
-    r = rows((ROWS, 2 * COLS)).astype(F32)
-    on_row = [target_row[i : i + 1] == r for i in (1, 2)]
-    c = lanes((2 * COLS, 2 * COLS))
-    gather = jnp.where(
-        rows((2 * COLS, 2 * COLS)) % FLUX == jnp.where(c < COLS, FLUX - 1, (c - COLS) // (2 * LEVELS)), 1.0, 0.0
-    ).astype(BF16)
-
-    level_of = (lane // 2) % LEVELS
-
-    def beside(i):
-        if i == 0:
-            x, own, way, own_wet = from_west, to_west, 1, to_west[:, 2 * FIELDS : 2 * FIELDS + 1]
-        else:
-            x, own, way, own_wet = from_east, to_east, -1, to_east[:, 2 * FIELDS + 1 : 2 * FIELDS + 2]
-        center = 2 * FIELDS + (1 - i)
-        wet_c = jnp.broadcast_to(x[:, center : center + 1], (ROWS, COLS))
-        wet_far = jnp.broadcast_to(x[:, center - way : center - way + 1], (ROWS, COLS))
-        wet_own = jnp.broadcast_to(own_wet, (ROWS, COLS))
-
-        def spread(at):
-            moved = [shift(x, 2 * (t * LEVELS - at), 1) for t in range(TRACERS)]
-            return jnp.where(lane < 2 * LEVELS, moved[0], jnp.where(lane < 4 * LEVELS, moved[1], moved[2]))
-
-        u, v = spread(EAST_AT), spread(NORTH_AT)
-        far, own = shift(x, way, 1), shift(own, way, 1)
-        plus, minus = jnp.maximum(u, 0.0), -jnp.minimum(u, 0.0)
-        c_far, c_own = (plus, minus) if i == 0 else (minus, plus)
-        change = (LATERAL * wet_far + c_far) * (far - x) + (LATERAL * wet_own + c_own) * (own - x)
-        step = shift(x, -2, 1) - x
-        return x, wet_c, v, change, step
-
-    halves = [beside(0), beside(1)]
+
+    for d in SENDS:
+        @pl.when(late[d])
+        def _():
+            pl.semaphore_wait(ack_sem.at[place_of[d]], 1)
+            if d in columns:
+                columns[d].start()
+            parts[d].start()
+
+    for copy in columns.values():
+        copy.wait_recv()
+    from_west, from_east = col_in[0, 0:ROWS], col_in[1, 0:ROWS]
+    from_both = jnp.where(lane % 2 == 1, from_west, from_east)
+
+    def to_edge(x, k):
+        return shift(x, -2 * k - 1, 1)
+
+    wet_outside = to_edge(from_both, FIELDS)
+    crossing = []
+    for level in range(LEVELS):
+        u = east_v[level]
+        speed = jnp.where(at_east, -jnp.minimum(u, 0.0), jnp.maximum(u, 0.0))
+        crossing.append(jnp.where(at_east | at_west, wet * (LATERAL * wet_outside + speed), 0.0))
+    for k in range(FIELDS):
+        where = pl.ds(k * ROWS, ROWS)
+        state_v[where, :] = state_v[where, :] + crossing[k % LEVELS] * (to_edge(from_both, k) - first[k])
+    for side, at in ((0, 0), (1, ROWS - 1)):
+        row_out[1, side, FIELDS : FIELDS + 1, :] = from_west[at : at + 1]
+        row_out[1, side, FIELDS + 1 : FIELDS + 2, :] = from_east[at : at + 1]
+        for i, x in enumerate((from_west, from_east)):
+            wet_corner = x[at : at + 1, 2 * FIELDS + 1 - i : 2 * FIELDS + 2 - i]
+            row_out[1, side, FIELDS + 2 + i : FIELDS + 3 + i, :] = jnp.broadcast_to(wet_corner, (1, COLS))
 
     for d in OFFSETS:
         parts[d].wait_recv()
@@ -351,13 +343,46 @@
 
     for side, at in ((0, 0), (1, ROWS - 1)):
         row_out[1, side, 0:FIELDS, :] = state_v[pl.ds(at, FIELDS, stride=ROWS), :]
-        row_out[1, side, FIELDS : FIELDS + 1, :] = from_west[at : at + 1]
-        row_out[1, side, FIELDS + 1 : FIELDS + 2, :] = from_east[at : at + 1]
-        row_out[1, side, FIELDS + 2 :, :] = jnp.zeros((2, COLS), F32)
     second_rows = row_copies(1)
-    for copy in second_rows.values():
-        copy.start()
-
+    for d, copy in second_rows.items():
+        @pl.when(there[d])
+        def _():
+            copy.start()
+
+    level_of = (lane // 2) % LEVELS
+
+    def beside(i):
+        if i == 0:
+            x, own, way, own_wet = from_west, to_west, 1, to_west[:, 2 * FIELDS : 2 * FIELDS + 1]
+        else:
+            x, own, way, own_wet = from_east, to_east, -1, to_east[:, 2 * FIELDS + 1 : 2 * FIELDS + 2]
+        center = 2 * FIELDS + (1 - i)
+        wet_c = jnp.broadcast_to(x[:, center : center + 1], (ROWS, COLS))
+        wet_far = jnp.broadcast_to(x[:, center - way : center - way + 1], (ROWS, COLS))
+        wet_own = jnp.broadcast_to(own_wet, (ROWS, COLS))
+
+        def spread(at):
+            moved = [shift(x, 2 * (t * LEVELS - at), 1) for t in range(TRACERS)]
+            return jnp.where(lane < 2 * LEVELS, moved[0], jnp.where(lane < 4 * LEVELS, moved[1], moved[2]))
+
+        u, v = spread(EAST_AT), spread(NORTH_AT)
+        far, own = shift(x, way, 1), shift(own, way, 1)
+        plus, minus = jnp.maximum(u, 0.0), -jnp.minimum(u, 0.0)
+        c_far, c_own = (plus, minus) if i == 0 else (minus, plus)
+        change = (LATERAL * wet_far + c_far) * (far - x) + (LATERAL * wet_own + c_own) * (own - x)
+        step = shift(x, -2, 1) - x
+        return x, wet_c, v, change, step
+
+    halves = [beside(0), beside(1)]
+
+    lists = jnp.where(edge_row == 0, col_in[0, ROWS:], col_in[1, ROWS:])
+    target_row = jnp.dot(lists.astype(BF16), expand, preferred_element_type=F32)
+    r = rows((ROWS, 2 * COLS)).astype(F32)
+    on_row = [target_row[i : i + 1] == r for i in (0, 1)]
+    c = lanes((2 * COLS, 2 * COLS))
+    gather = jnp.where(
+        rows((2 * COLS, 2 * COLS)) % FLUX == jnp.where(c < COLS, FLUX - 1, (c - COLS) // (2 * LEVELS)), 1.0, 0.0
+    ).astype(BF16)
     quarter = lanes((8, COLS)) // DATA
 
     def along_lanes(base, at):
@@ -389,44 +414,62 @@
         changes = (d01 + surface[t], d12 - d01, d23 - d12, -d23)
         for level, change in enumerate(changes):
             y = x[level]
-            near = (
-                jnp.where(at_east, 0.0, shift(y, -1, 1)),
-                jnp.where(at_west, 0.0, shift(y, 1, 1)),
-                jnp.where(at_north, 0.0, shift(y, -1, 0)),
-                jnp.where(at_south, 0.0, shift(y, 1, 0)),
+            north = jnp.where(at_north, 0.0, shift(y, -1, 0))
+            south = jnp.where(at_south, 0.0, shift(y, 1, 0))
+            new_o[pl.ds((t * LEVELS + level) * ROWS, ROWS), :] = (
+                lateral(y, level, north, south) - crossing[level] * y + change
             )
-            new_o[pl.ds((t * LEVELS + level) * ROWS, ROWS), :] = lateral(y, level, near) + change
-
-    for copy in second_rows.values():
-        copy.wait_recv()
+
+    halo, corner = [], []
+    for i, ((x, wet_c, v, _, _), change) in enumerate(zip(halves, inner)):
+        center = 2 * FIELDS + (1 - i)
+        wet_n, wet_s = shift(wet_c, -1, 0), shift(wet_c, 1, 0)
+        down_speed, up_speed = -jnp.minimum(v, 0.0), jnp.maximum(v, 0.0)
+        north = jnp.where(at_north, 0.0, (LATERAL * wet_n + down_speed) * (shift(x, -1, 0) - x))
+        south = jnp.where(at_south, 0.0, (LATERAL * wet_s + up_speed) * (shift(x, 1, 0) - x))
+        halo.append(x + wet_c * (change + north + south))
+        top_row, bottom_row = slice(ROWS - 1, ROWS), slice(0, 1)
+        corner.append((
+            (x[top_row], wet_c[top_row], down_speed[top_row]), (x[bottom_row], wet_c[bottom_row], up_speed[bottom_row])
+        ))
+    halo = jnp.where(lane % 2 == 1, halo[0], halo[1])
+    row8 = rows((8, COLS))
+    odd_lane = lanes((1, COLS)) % 2 == 1
+    ends = []
+    for level in range(LEVELS):
+        _, _, _, cn, cs = coefs[level]
+        cx = crossing[level]
+        ends.append((
+            jnp.where(row8 == 0, cx[0:8], 0.0), jnp.where(row8 == 7, cx[8:], 0.0),
+            jnp.where(row8 == 0, cs[0:8], 0.0), jnp.where(row8 == 7, cn[8:], 0.0),
+        ))
+    for k in range(FIELDS):
+        where = pl.ds(k * ROWS, ROWS)
+        new_o[where, :] = new_o[where, :] + crossing[k % LEVELS] * to_edge(halo, k)
+
+    for copy in (*parts.values(), *columns.values()):
+        copy.wait_send()
+    of_rows(first_rows, "send")
+    of_rows(second_rows, "recv")
     north_rows, south_rows = edges(1)
-    halo = []
-    for i, ((x, wet_c, v, _, _), change) in enumerate(zip(halves, inner)):
-        north = jnp.where(at_north, north_rows[FIELDS + i : FIELDS + i + 1], shift(x, -1, 0))
-        south = jnp.where(at_south, south_rows[FIELDS + i : FIELDS + i + 1], shift(x, 1, 0))
-        center = 2 * FIELDS + (1 - i)
-        wet_n = jnp.broadcast_to(north[:, center : center + 1], (ROWS, COLS))
-        wet_s = jnp.broadcast_to(south[:, center : center + 1], (ROWS, COLS))
-        change = change + (LATERAL * wet_n - jnp.minimum(v, 0.0)) * (north - x)
-        change = change + (LATERAL * wet_s + jnp.maximum(v, 0.0)) * (south - x)
-        halo.append(x + wet_c * change)
-    for level in range(LEVELS):
-        _, ce, cw, cn, cs = coefs[level]
-        ce, cw = jnp.where(at_east, ce, 0.0), jnp.where(at_west, cw, 0.0)
-        cn, cs = jnp.where(at_north, cn, 0.0), jnp.where(at_south, cs, 0.0)
-        for t in range(TRACERS):
-            k = t * LEVELS + level
-            where = pl.ds(k * ROWS, ROWS)
-            new_o[where, :] = (
-                new_o[where, :]
-                + cw * to_edge(halo[0], k, "west")
-                + ce * to_edge(halo[1], k, "east")
-                + cn * north_rows[k : k + 1]
-                + cs * south_rows[k : k + 1]
-            )
-
-    for copy in (*parts.values(), *first_rows.values(), *columns.values(), *second_rows.values()):
-        copy.wait_send()
+    lift = []
+    for side, beyond in ((0, north_rows), (1, south_rows)):
+        each = []
+        for i in range(2):
+            x, wet_c, speed = corner[i][side]
+            there_x = beyond[FIELDS + i : FIELDS + i + 1]
+            there_wet = beyond[FIELDS + 2 + i : FIELDS + 3 + i]
+            each.append(wet_c * (LATERAL * there_wet + speed) * (there_x - x))
+        lift.append(jnp.where(odd_lane, each[0], each[1]))
+    lift = jnp.where(row8 == 7, lift[0], lift[1])
+    for k in range(FIELDS):
+        x_low, x_high, c_low, c_high = ends[k % LEVELS]
+        low, high = pl.ds(k * ROWS, 8), pl.ds(k * ROWS + 8, 8)
+        moved = to_edge(lift, k)
+        new_o[low, :] = new_o[low, :] + x_low * moved + c_low * south_rows[k : k + 1]
+        new_o[high, :] = new_o[high, :] + x_high * moved + c_high * north_rows[k : k + 1]
+
+    of_rows(second_rows, "send")
 
 
 def store(ocean_v, new_v, ocean_o, new_o, sem):

time: 29.7 us -> 29.5 us (level)
  no operation moved by 1% of the time
where the time goes in v3:
time: 29.5 us; the launch traced here: 29.3 us
  Pallas kernels  28.7 us (97%)
  between operations  0.64 us (2%)
    pallas_call x1, Pallas kernels, body(): pl.pallas_call(kernel, out_shape=(jax.ShapeDtypeStruct((FLUX * ROWS, COLS...  28 us
    pallas_call x1, Pallas kernels, body(): pl.pallas_call(store, out_shape=(jax.ShapeDtypeStruct((FLUX * ROWS, COLS)...  0.67 us

profile of v3, /device:TPU:49, one launch (start us, length us, event | category | flops | bytes accessed | tf_op | source)
XLA Modules:
  0.0 29.3 jit_solution(10429963120928549634)
XLA Ops:
  0.6 28.0 %shard_map.104 = (f32[64,128]{1,0:T(8,128)S(1)}, f32[192,128]{1,0:T(8,128)S(1)}) custom-call(bf16[4,768]{1,0:T(4,128)(2,1)} %bitcast.7, bf16[56,128,128]{2,1,0:T(8,128)(2,1)} %bitcast.5, s32[1,56]{1,0:T(1,128)} %source_h.1, s32[1,7]{1,0:T(1,128)} %count_h.1, s32[1,56]{1,0:T(1,128)} %recv_h.1, s32[16,128]{1,0:T(8,128)} %land_h.1, f32[192,128]{1,0:T(8,128)} %bitcast.6, ...), custom_call_target="tpu_custom_call" | custom-call | tf_op jit(solution)/shard_map/pallas_call | solution.py:491
  28.7 0.7 %shard_map.105 = (f32[64,128]{1,0:T(8,128)}, f32[192,128]{1,0:T(8,128)}) custom-call(f32[64,128]{1,0:T(8,128)S(1)} %get-tuple-element.6.ocean_v, f32[192,128]{1,0:T(8,128)S(1)} %get-tuple-element.7.new_v), custom_call_target="tpu_custom_call" | custom-call | tf_op jit(solution)/shard_map/pallas_call | solution.py:541

commit v4 on v3

--- a/solution.py
+++ b/solution.py
@@ -122,29 +122,69 @@
     def shift(x, by, axis):
         return pltpu.roll(x, by % x.shape[axis], axis)
 
-    for name in ("flux", "source", "count", "tracer", "land", "place", "east", "north"):
+    for name in ("flux", "source", "count"):
         loads[name].wait()
     flux = flux_v[...].astype(F32)
     blocks = jnp.concatenate([flux[:, n * COLS : (n + 1) * COLS] for n in range(BLOCKS)], axis=0)
     blocks = jnp.concatenate([blocks, jnp.zeros((COLS - FLUX * BLOCKS, COLS), F32)], axis=0).astype(BF16)
+
+    def left(groups):
+        start, wide = min(groups) * DATA, len(groups) * DATA
+        at_slot = (rows((wide, SLOTS)) + start) // FLUX == lanes((wide, SLOTS))
+        at_group = (rows((wide, GROUPS)) + start) // DATA == lanes((wide, GROUPS))
+        source = jnp.where(at_slot, source_v[...].astype(F32), 0.0).astype(BF16)
+        count = jnp.where(at_group, count_v[...].astype(F32), 0.0).astype(BF16)
+        source = jnp.dot(source, jnp.ones((SLOTS, COLS), BF16), preferred_element_type=F32)
+        count = jnp.dot(count, jnp.ones((GROUPS, COLS), BF16), preferred_element_type=F32)
+        r, c = rows((wide, COLS)), lanes((wide, COLS))
+        pick = (
+            (source == (c // FLUX).astype(F32))
+            & (r % FLUX == c % FLUX)
+            & (((r // FLUX) % CAP).astype(F32) < count)
+        )
+        chosen = jnp.dot(jnp.where(pick, 1.0, 0.0).astype(BF16), blocks, preferred_element_type=F32)
+        low = r % 16 < 8
+        lhs_v[pl.ds(start, wide), 0:COLS] = jnp.where(low, chosen, 0.0).astype(BF16)
+        lhs_v[pl.ds(start, wide), COLS : 2 * COLS] = jnp.where(low, 0.0, chosen).astype(BF16)
+
     wide = FLUX * SLOTS
-    at_slot = rows((wide, SLOTS)) // FLUX == lanes((wide, SLOTS))
-    at_group = rows((wide, GROUPS)) // DATA == lanes((wide, GROUPS))
-    source = jnp.where(at_slot, source_v[...].astype(F32), 0.0).astype(BF16)
-    count = jnp.where(at_group, count_v[...].astype(F32), 0.0).astype(BF16)
-    source = jnp.dot(source, jnp.ones((SLOTS, COLS), BF16), preferred_element_type=F32)
-    count = jnp.dot(count, jnp.ones((GROUPS, COLS), BF16), preferred_element_type=F32)
-    r, c = rows((wide, COLS)), lanes((wide, COLS))
-    pick = (
-        (source == (c // FLUX).astype(F32))
-        & (r % FLUX == c % FLUX)
-        & (((r // FLUX) % CAP).astype(F32) < count)
-    )
-    chosen = jnp.dot(jnp.where(pick, 1.0, 0.0).astype(BF16), blocks, preferred_element_type=F32)
-    low = r % 16 < 8
-    lhs_v[:, 0:COLS] = jnp.where(low, chosen, 0.0).astype(BF16)
-    lhs_v[:, COLS : 2 * COLS] = jnp.where(low, 0.0, chosen).astype(BF16)
-
+
+    half = rows((16, COLS)) % 8 < 4
+    edge_row = rows((8, COLS))
+    ends = jnp.where(lanes((8, COLS)) == jnp.where(edge_row < 2, 0, COLS - 1), 1.0, 0.0).astype(BF16)
+    dims = (((1,), (1,)), ((), ()))
+
+    def split(x):
+        high = x.astype(BF16)
+        return high, (x - high.astype(F32)).astype(BF16)
+
+    def remap(groups):
+        for g in groups:
+            for q in (2 * g, 2 * g + 1):
+                w = [weight_v[4 * q + j] for j in range(4)]
+                tile = jnp.concatenate(
+                    [jnp.concatenate(w[0:2], axis=1), jnp.concatenate(w[2:4], axis=1)], axis=0
+                )
+                both = jnp.dot(lhs_v[pl.ds(16 * q, 16), :], tile, preferred_element_type=F32)
+                value = jnp.where(half, both[:, 0:COLS], both[:, COLS:])
+                part_v[pl.ds(16 * q, 16), :] = value
+                if g == REACH:
+                    recv_v[SPAN, pl.ds(16 * (q - 2 * g), 16), :] = value
+                else:
+                    send_v[g, pl.ds(16 * (q - 2 * g), 16), :] = value
+
+    def edge_columns(base, groups, at):
+        high, rest = split(part_v[pl.ds(base * DATA, COLS), :])
+        edge = lax.dot_general(ends, high, dims, preferred_element_type=F32)
+        edge = edge + lax.dot_general(ends, rest, dims, preferred_element_type=F32)
+        for g in groups:
+            send_v[g, DATA:, :] = edge
+        edge_v[at] = edge
+
+    left(AHEAD)
+    weights[AHEAD].wait()
+    for name in ("tracer", "land", "place", "east", "north"):
+        loads[name].wait()
     wet = land_v[...].astype(F32)
     first = [tracer_v[pl.ds(k * ROWS, ROWS), :] for k in range(FIELDS)]
     for side, at in ((0, 0), (1, ROWS - 1)):
@@ -164,39 +204,6 @@
         col_out[i, 0:ROWS, :] = value
         col_out[i, ROWS:, :] = margin
 
-    half = rows((16, COLS)) % 8 < 4
-    edge_row = rows((8, COLS))
-    ends = jnp.where(lanes((8, COLS)) == jnp.where(edge_row < 2, 0, COLS - 1), 1.0, 0.0).astype(BF16)
-    dims = (((1,), (1,)), ((), ()))
-
-    def split(x):
-        high = x.astype(BF16)
-        return high, (x - high.astype(F32)).astype(BF16)
-
-    def remap(groups):
-        weights[groups].wait()
-        for g in groups:
-            for q in (2 * g, 2 * g + 1):
-                w = [weight_v[4 * q + j] for j in range(4)]
-                tile = jnp.concatenate(
-                    [jnp.concatenate(w[0:2], axis=1), jnp.concatenate(w[2:4], axis=1)], axis=0
-                )
-                both = jnp.dot(lhs_v[pl.ds(16 * q, 16), :], tile, preferred_element_type=F32)
-                value = jnp.where(half, both[:, 0:COLS], both[:, COLS:])
-                part_v[pl.ds(16 * q, 16), :] = value
-                if g == REACH:
-                    recv_v[SPAN, pl.ds(16 * (q - 2 * g), 16), :] = value
-                else:
-                    send_v[g, pl.ds(16 * (q - 2 * g), 16), :] = value
-
-    def edge_columns(base, groups, at):
-        high, rest = split(part_v[pl.ds(base * DATA, COLS), :])
-        edge = lax.dot_general(ends, high, dims, preferred_element_type=F32)
-        edge = edge + lax.dot_general(ends, rest, dims, preferred_element_type=F32)
-        for g in groups:
-            send_v[g, DATA:, :] = edge
-        edge_v[at] = edge
-
     remap(AHEAD)
     edge_columns(REACH, AHEAD[:-1], 1)
 
@@ -214,11 +221,14 @@
     @pl.when(early[1])
     def _():
         columns[1].start()
+
     for d in SENDS[0:SPAN]:
         @pl.when(early[d])
         def _():
             parts[d].start()
 
+    left(BEHIND)
+    weights[BEHIND].wait()
     remap(BEHIND)
     edge_columns(0, BEHIND, 0)
 

time: 29.5 us -> 29.4 us (level)
  no operation moved by 1% of the time
where the time goes in v4:
time: 29.4 us; the launch traced here: 29.2 us
  Pallas kernels  28.6 us (97%)
  between operations  0.64 us (2%)
    pallas_call x1, Pallas kernels, body(): pl.pallas_call(kernel, out_shape=(jax.ShapeDtypeStruct((FLUX * ROWS, COLS...  27.9 us
    pallas_call x1, Pallas kernels, body(): pl.pallas_call(store, out_shape=(jax.ShapeDtypeStruct((FLUX * ROWS, COLS)...  0.67 us

profile of v4, /device:TPU:49, one launch (start us, length us, event | category | flops | bytes accessed | tf_op | source)
XLA Modules:
  0.0 29.2 jit_solution(10078228870543375332)
XLA Ops:
  0.6 27.9 %shard_map.104 = (f32[64,128]{1,0:T(8,128)S(1)}, f32[192,128]{1,0:T(8,128)S(1)}) custom-call(bf16[4,768]{1,0:T(4,128)(2,1)} %bitcast.7, bf16[56,128,128]{2,1,0:T(8,128)(2,1)} %bitcast.5, s32[1,56]{1,0:T(1,128)} %source_h.1, s32[1,7]{1,0:T(1,128)} %count_h.1, s32[1,56]{1,0:T(1,128)} %recv_h.1, s32[16,128]{1,0:T(8,128)} %land_h.1, f32[192,128]{1,0:T(8,128)} %bitcast.6, ...), custom_call_target="tpu_custom_call" | custom-call | tf_op jit(solution)/shard_map/pallas_call | solution.py:501
  28.5 0.7 %shard_map.105 = (f32[64,128]{1,0:T(8,128)}, f32[192,128]{1,0:T(8,128)}) custom-call(f32[64,128]{1,0:T(8,128)S(1)} %get-tuple-element.6.ocean_v, f32[192,128]{1,0:T(8,128)S(1)} %get-tuple-element.7.new_v), custom_call_target="tpu_custom_call" | custom-call | tf_op jit(solution)/shard_map/pallas_call | solution.py:551
